TPU v7x, 256 devices: a whole 4x4x8 slice. The times are simulated.
256 devices in a mesh: dp: 16 (over z_hi, y), expert: 16 (over z_lo, x, core).
Axes of the slice: x: 4, y: 4, z: 8 (z_hi: 4, z_lo: 2; z = z_hi * 2 + z_lo), core: 2. Of those that a mesh axis runs over, the one named last changes fastest.
Arguments:
- out_grad: bfloat16 [32768, 5120], P(('dp', 'expert')), may hold values from -6 to 6
- router_logits: float32 [32768, 16], P(('dp', 'expert')), may hold values from -5 to 303
- choice_ids: int32 [32768, 6], P(('dp', 'expert')), may hold values from 0 to 15, all different within a row; in each aligned block of 128 rows (0 to 127, 128 to 255, ...) at most 56 rows name the same one
- hidden: bfloat16 [16, 16, 16, 56, 768], P('dp', 'expert'), may hold values from -0.625 to 0.625
- master: float32 [768, 16, 5120], P('dp', 'expert'), may hold values from -0.21875 to 0.21875
- first: float32 [768, 16, 5120], P('dp', 'expert'), may hold values from -6 to 6
- second: float32 [768, 16, 5120], P('dp', 'expert'), may hold values from 0.1 to 10
Outputs:
- new_weight: float32 [768, 16, 5120], P('dp', 'expert')
- new_first: float32 [768, 16, 5120], P('dp', 'expert')
- new_second: float32 [768, 16, 5120], P('dp', 'expert')
- router_grad: float32 [32768, 16], P(('dp', 'expert'))
Inputs may be any that keep to these rules, and one draw needn't show every extreme that they name: `choice_ids`: each row names 6 different experts. In the rows of one device no expert is named more than 56 times, and in some device's rows some expert is named exactly 56 times.
All inputs are finite; a program needn't handle non-finite values.
Results may differ from a plain program's by a relative error of at most 0.0035.
Values may be sent and summed in bfloat16 or wider, within the bound.
A program may use at most 128 MiB of HBM per device.

v0:
```python
import jax
import jax.numpy as jnp
from jax import lax
from jax.sharding import PartitionSpec as P

beta_one = 0.9
beta_two = 0.95
learn_rate = 0.001
decay_rate = 0.1
epsilon = 1e-08
adam_step = 100.0


def pair_slots(choice_block, experts, capacity):
    tokens_here, picks = choice_block.shape
    flat_ids = choice_block.reshape(-1)
    labels = jnp.arange(experts, dtype=jnp.int32)
    onehot = (flat_ids[:, None] == labels[None, :]).astype(jnp.int32)
    earlier = jnp.cumsum(onehot, axis=0) - onehot
    slot_of = jnp.sum(earlier * onehot, axis=1)
    pair_index = jnp.arange(tokens_here * picks, dtype=jnp.int32)
    table = jnp.full((experts * capacity,), tokens_here * picks, jnp.int32)
    table = table.at[flat_ids * capacity + slot_of].set(pair_index)
    return (flat_ids, slot_of, table)


def shards(out_grad, router_logits, choice_ids, hidden, master, first, second):
    t_dev, width = out_grad.shape
    experts = router_logits.shape[1]
    topk = choice_ids.shape[1]
    sources = hidden.shape[2]
    capacity = hidden.shape[3]
    exp_dev = master.shape[1]
    probs = jax.nn.softmax(router_logits, axis=-1)
    flat_ids, slot_of, table = pair_slots(choice_ids, experts, capacity)
    pair_prob = jnp.take_along_axis(probs, choice_ids, axis=1).reshape(-1).astype(jnp.bfloat16)
    send_rows = jnp.take(out_grad, table // topk, axis=0, mode="fill", fill_value=0).reshape(
        experts, 1, capacity, width
    )
    send_prob = jnp.take(pair_prob, table, axis=0, mode="fill", fill_value=0).reshape(
        experts, 1, capacity
    )
    arrived, arrived_prob = (
        lax.all_to_all(send_rows, "expert", split_axis=0, concat_axis=1, tiled=True),
        lax.all_to_all(send_prob, "expert", split_axis=0, concat_axis=1, tiled=True),
    )
    rows = arrived.reshape(exp_dev, sources * capacity, width)
    row_prob = arrived_prob.reshape(exp_dev, sources * capacity)
    saved = hidden.reshape(exp_dev, sources * capacity, hidden.shape[4])
    weight_low = master.astype(jnp.bfloat16)
    scaled = (row_prob[:, :, None].astype(jnp.float32) * rows.astype(jnp.float32)).astype(
        jnp.bfloat16
    )
    back = jnp.einsum(
        "erd,fed->erf",
        rows,
        lax.all_gather(weight_low, "dp", axis=0, tiled=True),
        preferred_element_type=jnp.float32,
    )
    scores = jnp.sum(saved.astype(jnp.float32) * back, axis=2)
    grad = lax.psum_scatter(
        jnp.einsum("erf,erd->fed", saved, scaled, preferred_element_type=jnp.float32).astype(
            jnp.bfloat16
        ),
        "dp",
        scatter_dimension=0,
        tiled=True,
    ).astype(jnp.float32)
    returned = lax.all_to_all(
        scores.reshape(exp_dev, sources, capacity),
        "expert",
        split_axis=1,
        concat_axis=0,
        tiled=True,
    )
    pair_score = returned.reshape(-1)[flat_ids * capacity + slot_of].reshape(t_dev, topk)
    labels = jnp.arange(experts, dtype=jnp.int32)
    onehot = choice_ids[:, :, None] == labels[None, None, :]
    gain = jnp.sum(jnp.where(onehot, pair_score[:, :, None], 0.0), axis=1)
    router_grad = probs * (gain - jnp.sum(probs * gain, axis=1, keepdims=True))
    new_first = beta_one * first + (1.0 - beta_one) * grad
    new_second = beta_two * second + (1.0 - beta_two) * grad * grad
    first_hat = new_first / (1.0 - beta_one**adam_step)
    second_hat = new_second / (1.0 - beta_two**adam_step)
    new_weight = master - learn_rate * (
        first_hat / (jnp.sqrt(second_hat) + epsilon) + decay_rate * master
    )
    return (new_weight, new_first, new_second, router_grad)


def solution(mesh):
    return jax.shard_map(
        shards,
        mesh=mesh,
        in_specs=(
            P(("dp", "expert"), None),
            P(("dp", "expert"), None),
            P(("dp", "expert"), None),
            P("dp", "expert", None, None, None),
            P("dp", "expert", None),
            P("dp", "expert", None),
            P("dp", "expert", None),
        ),
        out_specs=(
            P("dp", "expert", None),
            P("dp", "expert", None),
            P("dp", "expert", None),
            P(("dp", "expert"), None),
        ),
        check_vma=False,
    )
```

profile of v0, /device:TPU:1, one launch (start us, length us, event | category | flops | bytes accessed | tf_op | source)
XLA Modules:
  0.0 1032.1 jit_solution(6347935586229452170)
XLA Ops:
  7.2 0.9 copy.70
  8.1 0.1 eq.42
  8.2 0.1 eq.38
  8.4 0.7 broadcast_multiply_fusion
  9.1 1.7 reduce-window.6
  10.8 0.3 slice_reduce_fusion
  11.1 0.1 copy.69
  11.2 0.1 mul.87
  11.3 0.1 fusion.19
  11.4 3.4 scatter_custom_fusion
  14.9 0.1 broadcast_in_dim.55
  15.0 7.8 gather_fusion.1
  22.8 7.8 broadcast_select_fusion
  30.6 7.9 all-to-all-start.1
  38.6 0.9 copy.101
  39.5 2.5 copy.83
  42.1 152.8 %all-gather.2.cloned.1.call-done = bf16[768,1,5120]{2,0,1:T(8,128)(2,1)} async-done(((bf16[48,1,5120]{2,0,1:T(8,128)(2,1)}), bf16[768,1,5120]{2,0,1:T(8,128)(2,1)}) %all-gather.2.cloned.1.call-update) | async-done | bytes 7864336 | tf_op jit(solution)/shard_map/all_gather | solution.py:57
  194.9 38.4 %all-to-all-done.1 = bf16[16,1,56,5120]{3,2,1,0:T(8,128)(2,1)} async-done(((bf16[16,1,56,5120]{3,2,1,0:T(8,128)(2,1)}), bf16[16,1,56,5120]{3,2,1,0:T(8,128)(2,1)}, u32[]{:S(2)}, u32[]{:S(2)}) %all-to-all-start.1) | async-done | bytes 9175072 | tf_op jit(solution)/shard_map/all_to_all | solution.py:44
  233.3 13.6 %multiply_reduce_fusion = f32[896]{0:T(1024)S(1)} fusion(bf16[896,768]{0,1:T(8,128)(2,1)} %copy.83, bf16[896,5120]{1,0:T(8,128)(2,1)} %bitcast.9, bf16[768,1,5120]{2,0,1:T(8,128)(2,1)} %all-gather.2.cloned.1.call-done), kind=kOutput, calls=%fused_computation.15 | convolution fusion | flops 7048494080 | bytes 18419200 | tf_op jit(solution)/shard_map/erd,fed->erf/dot_general | solution.py:54
  246.9 0.7 reshape.230
  247.6 14.0 %all-to-all-start.2 = ((f32[1,16,56]{2,0,1:T(1,128)}), f32[1,16,56]{2,0,1:T(1,128)S(1)}, u32[]{:S(2)}, u32[]{:S(2)}) async-start(f32[1,16,56]{2,0,1:T(1,128)} %reshape.230), calls=%async_computation.2 | async-start | bytes 16384 | tf_op jit(solution)/shard_map/all_to_all | solution.py:69
  261.6 0.1 copy.73
  261.8 0.1 reshape.258
  261.9 5.1 all-to-all-done.2
  267.0 0.5 broadcast.163
  267.5 0.7 reduce.13
  268.2 0.1 reshape.231
  268.3 3.2 gather_fusion.2
  271.5 0.1 broadcast_in_dim.59
  271.7 5.1 gather_fusion.3
  276.8 0.1 reshape.261
  277.1 0.1 copy.75
  277.2 0.2 convert_element_type.89
  277.4 5.8 gather_fusion
  283.2 0.1 select_n.73
  283.3 8.6 all_to_all.12
  291.9 0.1 reshape.232
  292.0 13.8 %fusion.10 = bf16[768,1,5120]{0,2,1:T(8,128)(2,1)} fusion(bf16[896,768]{1,0:T(8,128)(2,1)} %bitcast.53, bf16[1,896,1,1,1,1,5120]{6,1,5,4,3,2,0:T(8,128)(2,1)} %bitcast.12, f32[896]{0:T(1024)S(1)} %reshape.232), kind=kOutput, calls=%fused_computation.14 | convolution fusion | flops 7064125440 | bytes 18419200 | tf_op jit(solution)/shard_map/erf,erd->fed/dot_general | solution.py:62
  305.8 31.8 %copy.78 = bf16[768,1,5120]{2,1,0:T(2,128)(2,1)} copy(bf16[768,1,5120]{0,2,1:T(8,128)(2,1)} %fusion.10) | data formatting | bytes 15728640 | tf_op jit(solution)/shard_map/convert_element_type | solution.py:62
  337.7 0.6 copy-done.6
  338.3 0.6 dynamic-slice
  339.5 0.6 subtract_multiply_fusion
  340.1 674.7 %all-reduce.3.cloned.1.call-done = bf16[768,1,5120]{2,1,0:T(2,128)(2,1)} async-done(((bf16[768,1,5120]{2,1,0:T(2,128)(2,1)}), bf16[768,1,5120]{2,1,0:T(2,128)(2,1)}) %all-reduce.3.cloned.1.call-update) | async-done | bytes 7864336
  1014.9 2.2 constant_dynamic-slice_fusion
  1017.1 2.3 multiply_subtract_fusion
  1019.4 2.0 copy.86
  1021.4 2.0 copy.87
  1023.3 2.0 copy.88
  (36 shorter events, 0.5 us)
Async XLA Ops:
  7.2 7.8 copy-start
  30.6 7.9 copy-start.2
  30.6 11.4 %copy-start.5 = (f32[128,16]{0,1:T(8,128)S(1)}, f32[128,16]{0,1:T(8,128)}, u32[]{:S(2)}) copy-start(f32[128,16]{0,1:T(8,128)} %param.8) | copy-start | bytes 24580
  30.6 11.5 %copy-start.4 = (s32[128,6]{0,1:T(8,128)S(1)}, s32[128,6]{0,1:T(8,128)}, u32[]{:S(2)}) copy-start(s32[128,6]{0,1:T(8,128)} %param.9) | copy-start | bytes 9220
  30.6 202.7 %all-to-all-start.1 = ((bf16[16,1,56,5120]{3,2,1,0:T(8,128)(2,1)}), bf16[16,1,56,5120]{3,2,1,0:T(8,128)(2,1)}, u32[]{:S(2)}, u32[]{:S(2)}) async-start(bf16[16,1,56,5120]{3,2,1,0:T(8,128)(2,1)} %broadcast_select_fusion), calls=%async_computation.1 | async-start | bytes 18350080 | tf_op jit(solution)/shard_map/all_to_all | solution.py:44
  38.5 156.4 %all-gather.2.cloned.1.call-start = ((), (), s32[]{:S(2)}) async-start(), calls=%async_computation.3 | async-start | bytes 8355840 | tf_op jit(solution)/shard_map/all_gather | solution.py:57
  247.6 19.4 %all-to-all-start.2 = ((f32[1,16,56]{2,0,1:T(1,128)}), f32[1,16,56]{2,0,1:T(1,128)S(1)}, u32[]{:S(2)}, u32[]{:S(2)}) async-start(f32[1,16,56]{2,0,1:T(1,128)} %reshape.230), calls=%async_computation.2 | async-start | bytes 16384 | tf_op jit(solution)/shard_map/all_to_all | solution.py:69
  261.6 753.3 %all-reduce.3.cloned.1.call-start = ((), (), s32[]{:S(2)}) async-start(), calls=%async_computation.4 | async-start | bytes 31457280
  337.6 0.7 copy-start.6
  337.6 679.5 %copy-start.3 = (f32[48,1,5120]{2,1,0:T(1,128)S(1)}, f32[48,1,5120]{2,1,0:T(1,128)}, u32[]{:S(2)}) copy-start(f32[48,1,5120]{2,1,0:T(1,128)} %param.12) | copy-start | bytes 2949124
  337.6 687.6 %copy-start.1 = (bf16[128,5120]{1,0:T(8,128)(2,1)S(1)}, bf16[128,5120]{1,0:T(8,128)(2,1)}, u32[]{:S(2)}) copy-start(bf16[128,5120]{1,0:T(8,128)(2,1)} %param.7) | copy-start | bytes 3932164
Sparse Core Ops, SparseCore 0:
  42.3 152.5 all-gather.1
  337.8 677.0 all-reduce.2
where the time goes:
time: 1030 us
  waiting for transfers between devices  871 us (85%)
  local copies, waits for them, and re-layouts  74.1 us (7%)
  matrix products  27.3 us (3%)
  starting transfers between devices  21.9 us (2%)
  between operations  15 us (1%)
  other arithmetic  14.2 us (1%)
    unnamed x3, waiting for transfers between devices  675 us
    all_gather x1, waiting for transfers between devices, shards(): lax.all_gather(weight_low, 'dp', axis=0, tiled=True)  153 us
    all_to_all x1, waiting for transfers between devices, shards(): lax.all_to_all(send_rows, 'expert', split_axis=0, concat_axis=1, tiled=True)  38.4 us
    convert_element_type x1, local copies, waits for them, and re-layouts, shards(): jnp.einsum('erf,erd->fed', saved, scaled, preferred_element_type=jnp.floa...  31.8 us
  transfers between devices with their start and end apart: 4, of which 4 were waited for; matrix products, arithmetic and copies ran while one was open for 0% of the time, Pallas kernels for 0%

commit v1 on v0

v1 whole, which is shorter than its diff:
```python
import functools

import jax
import jax.numpy as jnp
from jax import lax
from jax.experimental import pallas as pl
from jax.experimental.pallas import tpu as pltpu
from jax.sharding import PartitionSpec as P

beta_one = 0.9
beta_two = 0.95
learn_rate = 0.001
decay_rate = 0.1
epsilon = 1e-08
adam_step = 100.0

MESH = pl.DeviceIdType.MESH
F32 = jnp.float32
BF16 = jnp.bfloat16

NZ, NY, NX = 4, 4, 4
PARTS = 10
KEEP = 4

Z_OWN, XP_OWN, XM_OWN, SIB_OWN = 0, 1, 2, 3
XP_PART, XM_PART, SIB_PART = 4, 5, 6
XP_FWD, XM_FWD = 7, 8
SIB_X = 9
SIB_F = 13
WZP, WZM, WZF, WYP, WYM, WYPF, WYMF = 15, 16, 17, 18, 19, 20, 21
FYP, FYM, RYP, RYM, FZP, FZM, RZP, RZM = 22, 23, 24, 25, 26, 27, 28, 29
KINDS = 30

LAG_C = 4


def kernel(
    og, ids, logits, hid, wl, grad_out, router_out,
    G, W, PB, FP, FM, RP, RM, S, ZFP, ZFM, ZRP, ZRM,
    HT, OH, ROWS, SCALED, ACC, CS, CR, GS, GR, PT,
    ss, rs, l1, l2, cs_s, cs_r, gs_s, gs_r,
):
    nc, experts, t_dev, C = G.shape
    rows_all, ff = hid.shape
    cap = rows_all // experts
    half = C // 2
    d = lax.axis_index("dp")
    e = lax.axis_index("expert")
    z, y = d // NY, d % NY
    zl, x, core = e // (2 * NX), (e // 2) % NX, e % 2
    up = lambda v: (v + 1) % 4
    down = lambda v: (v + 3) % 4
    opp = lambda v: (v + 2) % 4
    eid = lambda a, b, c: a * (2 * NX) + b * 2 + c
    did = lambda a, b: a * NY + b

    part = (d, eid(1 - zl, x, core))
    xp = (d, eid(zl, up(x), core))
    xm = (d, eid(zl, down(x), core))
    sib = (d, eid(zl, x, 1 - core))
    zp = (did(up(z), y), e)
    zm = (did(down(z), y), e)
    yp = (did(z, up(y)), e)
    ym = (did(z, down(y)), e)

    def rc(kind, j, src, dst, dev):
        return pltpu.make_async_remote_copy(
            src_ref=src, dst_ref=dst, send_sem=ss.at[kind, j], recv_sem=rs.at[kind, j],
            device_id=dev, device_id_type=MESH,
        )

    def cols(j, width=C):
        return pl.ds(pl.multiple_of(j * C, C), width)

    def local_g(j):
        return pltpu.make_async_copy(og.at[:, cols(j)], G.at[j, e], l1.at[j])

    def local_w(j):
        return pltpu.make_async_copy(wl.at[:, cols(j)], W.at[j, z, y], l2.at[j])

    def stage_local(j, carry):
        local_g(j).start()
        local_w(j).start()
        return carry

    lax.fori_loop(0, nc, stage_local, 0)

    barrier = pltpu.get_barrier_semaphore()

    def greet(k, carry):
        pl.semaphore_signal(barrier, inc=1, device_id=(d, (e + k) % experts), device_id_type=MESH)
        return carry

    lax.fori_loop(1, experts, greet, 0)
    for dev in (zp, zm, yp, ym):
        pl.semaphore_signal(barrier, inc=1, device_id=dev, device_id_type=MESH)
    pl.semaphore_wait(barrier, experts - 1 + 4)

    def block(j, a, b, c):
        return G.at[j, eid(a, b, c)]

    def d_send(kind, j, a, b, dev):
        ref = block(j, a, b, core)
        return rc(kind, j, ref, ref, dev)

    def d_recv(kind, j, a, b, c):
        ref = block(j, a, b, c)
        return rc(kind, j, ref, ref, sib)

    def w_copy(kind, j, ref, dev):
        return rc(kind, j, ref, ref, dev)

    def pslot(j):
        return j % KEEP

    def c_copy(peer, source):
        return pltpu.make_async_remote_copy(
            src_ref=CS.at[peer], dst_ref=CR.at[source], send_sem=cs_s.at[peer], recv_sem=cs_r.at[source],
            device_id=(d, peer), device_id_type=MESH,
        )

    def g_copy(peer, source):
        return pltpu.make_async_remote_copy(
            src_ref=GS.at[peer], dst_ref=GR.at[source], send_sem=gs_s.at[peer], recv_sem=gs_r.at[source],
            device_id=(d, peer), device_id_type=MESH,
        )

    def at_stage(i, lag, fn):
        j = i - lag

        @pl.when(jnp.logical_and(j >= 0, j < nc))
        def _():
            fn(j)

    def stage0(j):
        local_g(j).wait()
        local_w(j).wait()
        d_send(Z_OWN, j, zl, x, part).start()
        d_send(XP_OWN, j, zl, x, xp).start()
        d_send(XM_OWN, j, zl, x, xm).start()
        d_send(SIB_OWN, j, zl, x, sib).start()
        w_copy(WZP, j, W.at[j, z, y], zp).start()
        w_copy(WZM, j, W.at[j, z, y], zm).start()

    def stage1(j):
        d_recv(Z_OWN, j, 1 - zl, x, core).wait_recv()
        d_send(XP_PART, j, 1 - zl, x, xp).start()
        d_send(XM_PART, j, 1 - zl, x, xm).start()
        d_send(SIB_PART, j, 1 - zl, x, sib).start()
        w_copy(WZP, j, W.at[j, down(z), y], zp).wait_recv()
        w_copy(WZM, j, W.at[j, up(z), y], zm).wait_recv()

        @pl.when(j % 2 == 0)
        def _():
            w_copy(WZF, j, W.at[j, down(z), y], zp).start()

        @pl.when(j % 2 == 1)
        def _():
            w_copy(WZF, j, W.at[j, up(z), y], zm).start()

    def stage2(j):
        d_recv(XP_OWN, j, zl, down(x), core).wait_recv()
        d_recv(XM_OWN, j, zl, up(x), core).wait_recv()
        d_recv(XP_PART, j, 1 - zl, down(x), core).wait_recv()
        d_recv(XM_PART, j, 1 - zl, up(x), core).wait_recv()
        d_send(XP_FWD, j, 0, down(x), xp).start()
        d_send(XM_FWD, j, 1, up(x), xm).start()
        w_copy(WZF, j, W.at[j, opp(z), y], zp).wait_recv()
        w_copy(WYP, j, W.at[j, :, y], yp).start()
        w_copy(WYM, j, W.at[j, :, y], ym).start()
        for k, (a, b) in enumerate(((0, down(x)), (1, down(x)), (0, up(x)), (1, up(x)))):
            d_send(SIB_X + k, j, a, b, sib).start()

    def stage3(j):
        w_copy(WYP, j, W.at[j, :, down(y)], yp).wait_recv()
        w_copy(WYM, j, W.at[j, :, up(y)], ym).wait_recv()
        w_copy(WYPF, j, W.at[j, 0:2, down(y)], yp).start()
        w_copy(WYMF, j, W.at[j, 2:4, up(y)], ym).start()
        d_recv(XP_FWD, j, 0, opp(x), core).wait_recv()
        d_recv(XM_FWD, j, 1, opp(x), core).wait_recv()
        for k in range(2):
            d_send(SIB_F + k, j, k, opp(x), sib).start()

    def setup_select():
        def wait_code(k, carry):
            c_copy((e + k) % experts, (e + k) % experts).wait_recv()
            return carry

        lax.fori_loop(1, experts, wait_code, 0)
        CR[pl.ds(e, 1)] = CS[pl.ds(e, 1)]
        slots = lax.broadcasted_iota(jnp.int32, (cap, t_dev), 0).astype(F32)
        empty = jnp.zeros((cap, t_dev), F32)
        for p in range(experts // 2):
            one, weighted = [], []
            for s in range(2):
                tile = CR[2 * p + s]
                hot = jnp.where(slots == tile[0:1, :], 1.0, 0.0)
                gate = hot * tile[1:2, :]
                one.append(jnp.concatenate([hot, empty] if s == 0 else [empty, hot], axis=1))
                weighted.append(jnp.concatenate([gate, empty] if s == 0 else [empty, gate], axis=1))
            OH[p] = jnp.concatenate(one + weighted, axis=0).astype(BF16)

    def stage_c(j):
        @pl.when(j == 0)
        def _():
            setup_select()

        other = 1 - core
        d_recv(SIB_OWN, j, zl, x, other).wait_recv()
        d_recv(SIB_PART, j, 1 - zl, x, other).wait_recv()
        for k, (a, b) in enumerate(((0, down(x)), (1, down(x)), (0, up(x)), (1, up(x)))):
            d_recv(SIB_X + k, j, a, b, other).wait_recv()
        for k in range(2):
            d_recv(SIB_F + k, j, k, opp(x), other).wait_recv()

        pair = 2 * cap
        for p in range(experts // 2):
            tokens = G[j, 2 * p : 2 * p + 2].reshape(2 * t_dev, C)
            picked = jnp.dot(OH[p], tokens, preferred_element_type=F32)
            ROWS[p * pair : (p + 1) * pair, :] = picked[:pair].astype(BF16)
            SCALED[p * pair : (p + 1) * pair, :] = picked[pair:].astype(BF16)

        slot = pslot(j)

        @pl.when(j >= KEEP)
        def _():
            release(j - KEEP)

        partial = jnp.dot(HT[...], SCALED[...], preferred_element_type=F32)
        PB[slot] = partial.astype(BF16).reshape(NZ, NY, ff // (NZ * NY), C)
        rc(FYP, j, PB.at[slot, 2:4, opp(y)], FP.at[j], yp).start()
        rc(FYM, j, PB.at[slot, 0:2, opp(y)], FM.at[j], ym).start()

        w_copy(WYPF, j, W.at[j, 0:2, opp(y)], yp).wait_recv()
        w_copy(WYMF, j, W.at[j, 2:4, opp(y)], ym).wait_recv()
        through = jnp.dot(hid[...], W[j].reshape(ff, C), preferred_element_type=F32)
        product = through * ROWS[...].astype(F32)
        total = product[:, 0:128]
        for k in range(1, C // 128):
            total = total + product[:, k * 128 : (k + 1) * 128]
        ACC[...] += total

        @pl.when(j == nc - 1)
        def _():
            send_scores()

    def send_scores():
        score = jnp.sum(ACC[...], axis=1, keepdims=True)
        slots = lax.broadcasted_iota(jnp.int32, (cap, t_dev), 0).astype(F32)
        for s in range(experts):
            hot = slots == CR[s][0:1, :]
            GS[s, 0:1, :] = jnp.sum(
                jnp.where(hot, score[s * cap : (s + 1) * cap, :], 0.0), axis=0, keepdims=True
            )

        def send(k, carry):
            g_copy((e + k) % experts, e).start()
            return carry

        lax.fori_loop(1, experts, send, 0)
        GR[pl.ds(e, 1)] = GS[pl.ds(e, 1)]

    def release(j):
        slot = pslot(j)
        rc(FYP, j, PB.at[slot, 2:4, opp(y)], FP.at[j], yp).wait_send()
        rc(FYM, j, PB.at[slot, 0:2, opp(y)], FM.at[j], ym).wait_send()
        rc(RYP, j, PB.at[slot, :, up(y)], RP.at[j], yp).wait_send()
        rc(RYM, j, PB.at[slot, :, down(y)], RM.at[j], ym).wait_send()

    def stage_r1(j):
        slot = pslot(j)
        rc(FYP, j, PB.at[slot, 2:4, opp(y)], FP.at[j], yp).wait_recv()
        PB[slot, 2:4, up(y)] = (PB[slot, 2:4, up(y)].astype(F32) + FP[j].astype(F32)).astype(BF16)
        rc(RYP, j, PB.at[slot, :, up(y)], RP.at[j], yp).start()
        rc(FYM, j, PB.at[slot, 0:2, opp(y)], FM.at[j], ym).wait_recv()
        PB[slot, 0:2, down(y)] = (PB[slot, 0:2, down(y)].astype(F32) + FM[j].astype(F32)).astype(BF16)
        rc(RYM, j, PB.at[slot, :, down(y)], RM.at[j], ym).start()

    def stage_r2(j):
        slot = pslot(j)
        rc(RYP, j, PB.at[slot, :, up(y)], RP.at[j], yp).wait_recv()
        rc(RYM, j, PB.at[slot, :, down(y)], RM.at[j], ym).wait_recv()
        S[j] = (PB[slot, :, y].astype(F32) + RP[j].astype(F32) + RM[j].astype(F32)).astype(BF16)
        rc(FZP, j, S.at[j, opp(z), :, 0:half], ZFP.at[j], zp).start()
        rc(FZM, j, S.at[j, opp(z), :, half:C], ZFM.at[j], zm).start()

    def stage_r3(j):
        rc(FZP, j, S.at[j, opp(z), :, 0:half], ZFP.at[j], zp).wait_recv()
        S[j, up(z), :, 0:half] = (S[j, up(z), :, 0:half].astype(F32) + ZFP[j].astype(F32)).astype(BF16)
        rc(RZP, j, S.at[j, up(z)], ZRP.at[j], zp).start()
        rc(FZM, j, S.at[j, opp(z), :, half:C], ZFM.at[j], zm).wait_recv()
        S[j, down(z), :, half:C] = (S[j, down(z), :, half:C].astype(F32) + ZFM[j].astype(F32)).astype(BF16)
        rc(RZM, j, S.at[j, down(z)], ZRM.at[j], zm).start()

    def stage_r4(j):
        rc(RZP, j, S.at[j, up(z)], ZRP.at[j], zp).wait_recv()
        rc(RZM, j, S.at[j, down(z)], ZRM.at[j], zm).wait_recv()
        grad_out[:, cols(j)] = S[j, z].astype(F32) + ZRP[j].astype(F32) + ZRM[j].astype(F32)

    lanes = lax.broadcasted_iota(jnp.int32, (t_dev, experts), 1)
    chosen = jnp.zeros((t_dev, experts), F32)
    for k in range(ids.shape[1]):
        chosen = chosen + jnp.where(ids[:, k : k + 1] == lanes, 1.0, 0.0)
    row = lax.broadcasted_iota(jnp.int32, (t_dev, t_dev), 0)
    col = lax.broadcasted_iota(jnp.int32, (t_dev, t_dev), 1)
    earlier = jnp.where(col < row, 1.0, 0.0).astype(BF16)
    slot_of = jnp.dot(earlier, chosen.astype(BF16), preferred_element_type=F32)
    code = jnp.where(chosen > 0.5, slot_of, -1.0)
    scores = logits[...]
    powers = jnp.exp(scores - jnp.max(scores, axis=1, keepdims=True))
    probs = powers / jnp.sum(powers, axis=1, keepdims=True)
    code_t = code.T
    probs_t = probs.T
    PT[...] = probs_t
    gate_t = probs_t.astype(BF16).astype(F32)
    CS[...] = jnp.zeros_like(CS)
    GS[...] = jnp.zeros_like(GS)
    ACC[...] = jnp.zeros_like(ACC)
    for s in range(experts):
        CS[s, 0:1, :] = code_t[s : s + 1, :]
        CS[s, 1:2, :] = gate_t[s : s + 1, :]

    def send_code(k, carry):
        c_copy((e + k) % experts, e).start()
        return carry

    stage0(0)
    lax.fori_loop(1, experts, send_code, 0)
    HT[...] = hid[...].T

    def tick(i, carry):
        at_stage(i, LAG_C + 1, stage_r1)
        at_stage(i, LAG_C + 2, stage_r2)
        at_stage(i, LAG_C + 3, stage_r3)
        at_stage(i, LAG_C + 4, stage_r4)

        @pl.when(jnp.logical_and(i > 0, i < nc))
        def _():
            stage0(i)

        at_stage(i, 1, stage1)
        at_stage(i, 2, stage2)
        at_stage(i, 3, stage3)
        at_stage(i, LAG_C, stage_c)
        return carry

    lax.fori_loop(0, nc + LAG_C + 4, tick, 0)

    def wait_gain(k, carry):
        peer = (e + k) % experts
        g_copy(peer, peer).wait_recv()
        return carry

    lax.fori_loop(1, experts, wait_gain, 0)
    gain = jnp.concatenate([GR[s][0:1, :] for s in range(experts)], axis=0)
    probs_t = PT[...]
    router_t = probs_t * (gain - jnp.sum(probs_t * gain, axis=0, keepdims=True))
    router_out[...] = router_t.T

    def drain(j, carry):
        ref = block(j, zl, x, core)
        for kind in range(SIB_F + 2):
            rc(kind, j, ref, ref, sib).wait_send()
        ref = W.at[j, z, y]
        for kind in (WZP, WZM, WZF):
            rc(kind, j, ref, ref, zp).wait_send()
        for kind in (WYP, WYM):
            rc(kind, j, W.at[j, :, y], W.at[j, :, y], yp).wait_send()
        for kind in (WYPF, WYMF):
            rc(kind, j, W.at[j, 0:2, y], W.at[j, 0:2, y], yp).wait_send()
        rc(FZP, j, S.at[j, opp(z), :, 0:half], ZFP.at[j], zp).wait_send()
        rc(FZM, j, S.at[j, opp(z), :, half:C], ZFM.at[j], zm).wait_send()
        rc(RZP, j, S.at[j, up(z)], ZRP.at[j], zp).wait_send()
        rc(RZM, j, S.at[j, down(z)], ZRM.at[j], zm).wait_send()

        @pl.when(j >= nc - KEEP)
        def _():
            release(j)

        return carry

    lax.fori_loop(0, nc, drain, 0)

    def drain_small(k, carry):
        peer = (e + k) % experts
        c_copy(peer, e).wait_send()
        g_copy(peer, e).wait_send()
        return carry

    lax.fori_loop(1, experts, drain_small, 0)


def exchange(out_grad, router_logits, choice_ids, saved, weight_low):
    t_dev, width = out_grad.shape
    experts = router_logits.shape[1]
    rows_all, ff = saved.shape
    own = weight_low.shape[0]
    nc = PARTS
    C = width // nc
    vm = pl.BlockSpec(memory_space=pltpu.VMEM)
    hbm = pl.BlockSpec(memory_space=pl.ANY)
    dma = pltpu.SemaphoreType.DMA
    return pl.pallas_call(
        kernel,
        out_shape=(
            jax.ShapeDtypeStruct((own, width), F32),
            jax.ShapeDtypeStruct((t_dev, experts), F32),
        ),
        in_specs=[hbm, vm, vm, vm, hbm],
        out_specs=(vm, vm),
        scratch_shapes=[
            pltpu.VMEM((nc, experts, t_dev, C), BF16),
            pltpu.VMEM((nc, NZ, NY, own, C), BF16),
            pltpu.VMEM((KEEP, NZ, NY, own, C), BF16),
            pltpu.VMEM((nc, 2, own, C), BF16),
            pltpu.VMEM((nc, 2, own, C), BF16),
            pltpu.VMEM((nc, NZ, own, C), BF16),
            pltpu.VMEM((nc, NZ, own, C), BF16),
            pltpu.VMEM((nc, NZ, own, C), BF16),
            pltpu.VMEM((nc, own, C // 2), BF16),
            pltpu.VMEM((nc, own, C // 2), BF16),
            pltpu.VMEM((nc, own, C), BF16),
            pltpu.VMEM((nc, own, C), BF16),
            pltpu.VMEM((ff, rows_all), BF16),
            pltpu.VMEM((experts // 2, 4 * (rows_all // experts), 2 * t_dev), BF16),
            pltpu.VMEM((rows_all, C), BF16),
            pltpu.VMEM((rows_all, C), BF16),
            pltpu.VMEM((rows_all, 128), F32),
            pltpu.VMEM((experts, 8, t_dev), F32),
            pltpu.VMEM((experts, 8, t_dev), F32),
            pltpu.VMEM((experts, 8, t_dev), F32),
            pltpu.VMEM((experts, 8, t_dev), F32),
            pltpu.VMEM((experts, t_dev), F32),
            dma((KINDS, nc)),
            dma((KINDS, nc)),
            dma((nc,)),
            dma((nc,)),
            dma((experts,)),
            dma((experts,)),
            dma((experts,)),
            dma((experts,)),
        ],
        compiler_params=pltpu.CompilerParams(
            collective_id=0, has_side_effects=True, vmem_limit_bytes=62 * 1024 * 1024
        ),
    )(out_grad, choice_ids, router_logits, saved, weight_low)


def shards(out_grad, router_logits, choice_ids, hidden, master, first, second):
    own, _, width = master.shape
    saved = hidden.reshape(hidden.shape[2] * hidden.shape[3], hidden.shape[4])
    weight_low = master.astype(BF16).reshape(own, width)
    grad, router_grad = exchange(out_grad, router_logits, choice_ids, saved, weight_low)
    grad = grad.reshape(own, 1, width)
    new_first = beta_one * first + (1.0 - beta_one) * grad
    new_second = beta_two * second + (1.0 - beta_two) * grad * grad
    first_hat = new_first / (1.0 - beta_one**adam_step)
    second_hat = new_second / (1.0 - beta_two**adam_step)
    new_weight = master - learn_rate * (
        first_hat / (jnp.sqrt(second_hat) + epsilon) + decay_rate * master
    )
    return (new_weight, new_first, new_second, router_grad)


def solution(mesh):
    return jax.shard_map(
        shards,
        mesh=mesh,
        in_specs=(
            P(("dp", "expert"), None),
            P(("dp", "expert"), None),
            P(("dp", "expert"), None),
            P("dp", "expert", None, None, None),
            P("dp", "expert", None),
            P("dp", "expert", None),
            P("dp", "expert", None),
        ),
        out_specs=(
            P("dp", "expert", None),
            P("dp", "expert", None),
            P("dp", "expert", None),
            P(("dp", "expert"), None),
        ),
        check_vma=False,
    )
```

time: 1030 us -> 200 us (0.19)
  the two profiles are of different devices: /device:TPU:1 before, /device:TPU:48 now
where the time goes in v1:
time: 200 us; the launch traced here: 199 us
  Pallas kernels  184 us (92%)
  local copies, waits for them, and re-layouts  12.4 us (6%)
  other arithmetic  2.47 us (1%)
    pallas_call x1, Pallas kernels, exchange(): pl.pallas_call(kernel, out_shape=(jax.ShapeDtypeStruct((own, width), F32)...  184 us
    unnamed x11, local copies, waits for them, and re-layouts  12.4 us

profile of v1, /device:TPU:48, one launch (start us, length us, event | category | flops | bytes accessed | tf_op | source)
XLA Modules:
  0.0 199.4 jit_solution(94073988653265294)
XLA Ops:
  0.6 1.4 copy.14.logits
  2.1 1.4 copy.13.ids
  3.5 2.1 %copy.34 = bf16[48,1,5120]{2,0,1:T(8,128)(2,1)} copy(f32[48,1,5120]{2,1,0:T(1,128)} %param.11) | data formatting | bytes 1474560 | tf_op args[4]
  5.6 0.0 copy-start
  5.6 0.0 copy-start.1
  5.6 183.9 %shard_map.102 = (f32[48,5120]{1,0:T(8,128)}, f32[128,16]{1,0:T(8,128)}) custom-call(bf16[128,5120]{1,0:T(8,128)(2,1)} %og.1, s32[128,6]{1,0:T(8,128)} %copy.13.ids, f32[128,16]{1,0:T(8,128)} %copy.14.logits, bf16[896,768]{1,0:T(8,128)(2,1)} %bitcast.13, bf16[48,5120]{1,0:T(8,128)(2,1)} %bitcast.12), custom_call_target="tpu_custom_call" | custom-call | tf_op jit(solution)/shard_map/pallas_call | solution.py:403
  189.6 1.5 copy.21
  191.1 0.0 copy-done
  191.1 0.0 copy-done.1
  191.1 2.5 %multiply_subtract_fusion = (f32[48,1,5120]{2,0,1:T(8,128)S(1)}, f32[48,1,5120]{2,0,1:T(8,128)S(1)}, f32[48,1,5120]{2,0,1:T(8,128)S(1)}) fusion(f32[48,1,5120]{2,1,0:T(1,128)S(1)} %copy-done, f32[48,5120]{1,0:T(8,128)} %get-tuple-element.6, f32[48,1,5120]{2,1,0:T(1,128)S(1)} %copy-done.1, f32[48,1,5120]{2,1,0:T(1,128)} %param.13), kind=kLoop, calls=%fused_computation.6 | loop fusion | flops 3686400 | bytes 6881280 | tf_op jit(solution)/shard_map/sub | solution.py:459
  193.6 2.0 copy.18
  195.5 2.0 copy.19
  197.5 2.0 copy.20
Async XLA Ops:
  5.6 185.5 %copy-start = (f32[48,1,5120]{2,1,0:T(1,128)S(1)}, f32[48,1,5120]{2,1,0:T(1,128)}, u32[]{:S(2)}) copy-start(f32[48,1,5120]{2,1,0:T(1,128)} %param.11) | copy-start | bytes 2949124
  5.6 185.5 %copy-start.1 = (f32[48,1,5120]{2,1,0:T(1,128)S(1)}, f32[48,1,5120]{2,1,0:T(1,128)}, u32[]{:S(2)}) copy-start(f32[48,1,5120]{2,1,0:T(1,128)} %param.12) | copy-start | bytes 2949124

commit v2 on v1

v2 whole, which is shorter than its diff:
```python
import functools

import jax
import jax.numpy as jnp
from jax import lax
from jax.experimental import pallas as pl
from jax.experimental.pallas import tpu as pltpu
from jax.sharding import PartitionSpec as P

beta_one = 0.9
beta_two = 0.95
learn_rate = 0.001
decay_rate = 0.1
epsilon = 1e-08
adam_step = 100.0

MESH = pl.DeviceIdType.MESH
F32 = jnp.float32
BF16 = jnp.bfloat16

NZ, NY, NX = 4, 4, 4
PARTS = 20
HOP = 2
KEEP = 2 * HOP + 2

Z_OWN, XP_OWN, XM_OWN, SIB_OWN = 0, 1, 2, 3
XP_PART, XM_PART, SIB_PART = 4, 5, 6
XP_FWD, XM_FWD = 7, 8
SIB_X = 9
SIB_F = 13
WZ, WZF, WY, WYF, SF, SR = 15, 16, 17, 18, 19, 20
SENDS = 21

(R_Z, R_X, R_XF, R_SIB, R_WZ, R_WZF, R_WY, R_WYF, R_FY, R_RY, R_FZ, R_RZ) = range(12)
RECVS = 12


def kernel(
    og, ids, logits, hid_in, master_in, grad_out, router_out,
    G, W, PB, FY, RY, S, FZ, RZ,
    hid, master, HT, OH, ROWS, SCALED, ACC, CS, CR, GS, GR, PT,
    ss, rs, ps, l1, l2, cs_s, cs_r, gs_s, gs_r,
):
    nc, experts, t_dev, C = G.shape
    rows_all, ff = hid.shape
    cap = rows_all // experts
    half = C // 2
    d = lax.axis_index("dp")
    e = lax.axis_index("expert")
    z, y = d // NY, d % NY
    zl, x, core = e // (2 * NX), (e // 2) % NX, e % 2
    up = lambda v: (v + 1) % 4
    down = lambda v: (v + 3) % 4
    opp = lambda v: (v + 2) % 4
    eid = lambda a, b, c: a * (2 * NX) + b * 2 + c
    did = lambda a, b: a * NY + b

    part = (d, eid(1 - zl, x, core))
    xp = (d, eid(zl, up(x), core))
    xm = (d, eid(zl, down(x), core))
    sib = (d, eid(zl, x, 1 - core))
    zp = (did(up(z), y), e)
    zm = (did(down(z), y), e)
    yp = (did(z, up(y)), e)
    ym = (did(z, down(y)), e)

    def rc(send, recv, src, dst, dev):
        return pltpu.make_async_remote_copy(
            src_ref=src, dst_ref=dst, send_sem=send, recv_sem=recv, device_id=dev, device_id_type=MESH
        )

    def arrive(recv, j, ref):
        rc(ss.at[0], rs.at[recv, j], ref, ref, sib).wait_recv()

    def left(send, ref):
        rc(send, rs.at[0, 0], ref, ref, sib).wait_send()

    def cols(j, width=C):
        return pl.ds(pl.multiple_of(j * C, C), width)

    def local_g(j):
        return pltpu.make_async_copy(og.at[:, cols(j)], G.at[j, e], l1.at[j])

    own, lanes_of = W.shape[3], nc * C // 128

    def flat(j, k):
        return pl.ds(j * (C // 128) + k, own, stride=lanes_of)

    def stage_local(j, carry):
        local_g(j).start()
        return carry

    load_master = pltpu.make_async_copy(master_in, master, l2.at[0])
    load_hidden = pltpu.make_async_copy(hid_in, hid, l2.at[1])
    load_master.start()
    lax.fori_loop(0, nc, stage_local, 0)
    load_hidden.start()

    barrier = pltpu.get_barrier_semaphore()

    def greet(k, carry):
        pl.semaphore_signal(barrier, inc=1, device_id=(d, (e + k) % experts), device_id_type=MESH)
        return carry

    lax.fori_loop(1, experts, greet, 0)
    for dev in (zp, zm, yp, ym):
        pl.semaphore_signal(barrier, inc=1, device_id=dev, device_id_type=MESH)
    pl.semaphore_wait(barrier, experts - 1 + 4)

    def send_d(kind, recv, j, a, b, dev):
        ref = G.at[j, eid(a, b, core)]
        rc(ss.at[kind], rs.at[recv, j], ref, ref, dev).start()

    def send_w(kind, recv, j, ref, dev):
        rc(ss.at[kind], rs.at[recv, j], ref, ref, dev).start()

    def pslot(j):
        return j % KEEP

    def c_copy(peer, source):
        return pltpu.make_async_remote_copy(
            src_ref=CS.at[peer], dst_ref=CR.at[source], send_sem=cs_s.at[peer], recv_sem=cs_r.at[source],
            device_id=(d, peer), device_id_type=MESH,
        )

    def g_copy(peer, source):
        return pltpu.make_async_remote_copy(
            src_ref=GS.at[peer], dst_ref=GR.at[source], send_sem=gs_s.at[peer], recv_sem=gs_r.at[source],
            device_id=(d, peer), device_id_type=MESH,
        )

    def at_stage(i, lag, fn):
        j = i - lag

        @pl.when(jnp.logical_and(j >= 0, j < nc))
        def _():
            fn(j)

    def stage0(j):
        local_g(j).wait()
        for k in range(C // 128):
            W[j, z, y, :, k * 128 : (k + 1) * 128] = master[flat(j, k), :].astype(BF16)
        send_d(Z_OWN, R_Z, j, zl, x, part)
        send_d(XP_OWN, R_X, j, zl, x, xp)
        send_d(XM_OWN, R_X, j, zl, x, xm)
        send_d(SIB_OWN, R_SIB, j, zl, x, sib)
        send_w(WZ, R_WZ, j, W.at[j, z, y], zp)
        send_w(WZ, R_WZ, j, W.at[j, z, y], zm)

    def stage1(j):
        arrive(R_Z, j, G.at[j, 0])
        send_d(XP_PART, R_X, j, 1 - zl, x, xp)
        send_d(XM_PART, R_X, j, 1 - zl, x, xm)
        send_d(SIB_PART, R_SIB, j, 1 - zl, x, sib)
        arrive(R_WZ, j, W.at[j, 0, 0:2])

        @pl.when(j % 2 == 0)
        def _():
            send_w(WZF, R_WZF, j, W.at[j, down(z), y], zp)

        @pl.when(j % 2 == 1)
        def _():
            send_w(WZF, R_WZF, j, W.at[j, up(z), y], zm)

    def stage2(j):
        arrive(R_X, j, G.at[j, 0:4])
        send_d(XP_FWD, R_XF, j, 0, down(x), xp)
        send_d(XM_FWD, R_XF, j, 1, up(x), xm)
        arrive(R_WZF, j, W.at[j, 0, 0])
        send_w(WY, R_WY, j, W.at[j, :, y], yp)
        send_w(WY, R_WY, j, W.at[j, :, y], ym)
        for k, (a, b) in enumerate(((0, down(x)), (1, down(x)), (0, up(x)), (1, up(x)))):
            send_d(SIB_X + k, R_SIB, j, a, b, sib)

    def stage3(j):
        arrive(R_WY, j, W.at[j, 0:2])
        send_w(WYF, R_WYF, j, W.at[j, 0:2, down(y)], yp)
        send_w(WYF, R_WYF, j, W.at[j, 2:4, up(y)], ym)
        arrive(R_XF, j, G.at[j, 0:2])
        for k in range(2):
            send_d(SIB_F + k, R_SIB, j, k, opp(x), sib)

    def setup_select():
        def wait_code(k, carry):
            c_copy((e + k) % experts, (e + k) % experts).wait_recv()
            return carry

        lax.fori_loop(1, experts, wait_code, 0)
        CR[pl.ds(e, 1)] = CS[pl.ds(e, 1)]
        slots = lax.broadcasted_iota(jnp.int32, (cap, t_dev), 0).astype(F32)
        empty = jnp.zeros((cap, t_dev), F32)
        for p in range(experts // 2):
            one, weighted = [], []
            for s in range(2):
                tile = CR[2 * p + s]
                hot = jnp.where(slots == tile[0:1, :], 1.0, 0.0)
                gate = hot * tile[1:2, :]
                one.append(jnp.concatenate([hot, empty] if s == 0 else [empty, hot], axis=1))
                weighted.append(jnp.concatenate([gate, empty] if s == 0 else [empty, gate], axis=1))
            OH[p] = jnp.concatenate(one + weighted, axis=0).astype(BF16)

    def stage_c(j):
        @pl.when(j == 0)
        def _():
            setup_select()

        arrive(R_SIB, j, G.at[j, 0:8])

        pair = 2 * cap
        for p in range(experts // 2):
            tokens = G[j, 2 * p : 2 * p + 2].reshape(2 * t_dev, C)
            picked = jnp.dot(OH[p], tokens, preferred_element_type=F32)
            ROWS[p * pair : (p + 1) * pair, :] = picked[:pair].astype(BF16)
            SCALED[p * pair : (p + 1) * pair, :] = picked[pair:].astype(BF16)

        slot = pslot(j)

        @pl.when(j >= KEEP)
        def _():
            release(j - KEEP)

        partial = jnp.dot(HT[...], SCALED[...], preferred_element_type=F32)
        PB[slot] = partial.astype(BF16).reshape(NZ, NY, ff // (NZ * NY), C)
        rc(ps.at[slot], rs.at[R_FY, j], PB.at[slot, 2:4, opp(y)], FY.at[j, 0], yp).start()
        rc(ps.at[slot], rs.at[R_FY, j], PB.at[slot, 0:2, opp(y)], FY.at[j, 1], ym).start()

        arrive(R_WYF, j, W.at[j, 0])
        through = jnp.dot(hid[...], W[j].reshape(ff, C), preferred_element_type=F32)
        product = through * ROWS[...].astype(F32)
        total = product[:, 0:128]
        for k in range(1, C // 128):
            total = total + product[:, k * 128 : (k + 1) * 128]
        ACC[...] += total

        @pl.when(j == nc - 1)
        def _():
            send_scores()

    def send_scores():
        score = jnp.sum(ACC[...], axis=1, keepdims=True)
        slots = lax.broadcasted_iota(jnp.int32, (cap, t_dev), 0).astype(F32)
        for s in range(experts):
            hot = slots == CR[s][0:1, :]
            GS[s, 0:1, :] = jnp.sum(
                jnp.where(hot, score[s * cap : (s + 1) * cap, :], 0.0), axis=0, keepdims=True
            )

        def send(k, carry):
            g_copy((e + k) % experts, e).start()
            return carry

        lax.fori_loop(1, experts, send, 0)
        GR[pl.ds(e, 1)] = GS[pl.ds(e, 1)]

    def release(j):
        slot = pslot(j)
        left(ps.at[slot], PB.at[slot, 0:3])

    def add(a, b):
        return (a.astype(F32) + b.astype(F32)).astype(BF16)

    def stage_r1(j):
        slot = pslot(j)
        arrive(R_FY, j, FY.at[j])
        PB[slot, 2:4, up(y)] = add(PB[slot, 2:4, up(y)], FY[j, 0])
        rc(ps.at[slot], rs.at[R_RY, j], PB.at[slot, :, up(y)], RY.at[j, 0], yp).start()
        PB[slot, 0:2, down(y)] = add(PB[slot, 0:2, down(y)], FY[j, 1])
        rc(ps.at[slot], rs.at[R_RY, j], PB.at[slot, :, down(y)], RY.at[j, 1], ym).start()

    def stage_r2(j):
        slot = pslot(j)
        arrive(R_RY, j, RY.at[j])
        S[j] = (PB[slot, :, y].astype(F32) + RY[j, 0].astype(F32) + RY[j, 1].astype(F32)).astype(BF16)
        rc(ss.at[SF], rs.at[R_FZ, j], S.at[j, opp(z), :, 0:half], FZ.at[j, 0], zp).start()
        rc(ss.at[SF], rs.at[R_FZ, j], S.at[j, opp(z), :, half:C], FZ.at[j, 1], zm).start()

    def stage_r3(j):
        arrive(R_FZ, j, FZ.at[j])
        S[j, up(z), :, 0:half] = add(S[j, up(z), :, 0:half], FZ[j, 0])
        rc(ss.at[SR], rs.at[R_RZ, j], S.at[j, up(z)], RZ.at[j, 0], zp).start()
        S[j, down(z), :, half:C] = add(S[j, down(z), :, half:C], FZ[j, 1])
        rc(ss.at[SR], rs.at[R_RZ, j], S.at[j, down(z)], RZ.at[j, 1], zm).start()

    def stage_r4(j):
        arrive(R_RZ, j, RZ.at[j])
        total = S[j, z].astype(F32) + RZ[j, 0].astype(F32) + RZ[j, 1].astype(F32)
        for k in range(C // 128):
            grad_out[flat(j, k), :] = total[:, k * 128 : (k + 1) * 128]

    labels = lax.broadcasted_iota(jnp.int32, (experts, t_dev), 0)
    chosen = jnp.zeros((experts, t_dev), F32)
    for k in range(ids.shape[0]):
        chosen = chosen + jnp.where(ids[k : k + 1, :] == labels, 1.0, 0.0)
    row = lax.broadcasted_iota(jnp.int32, (t_dev, t_dev), 0)
    col = lax.broadcasted_iota(jnp.int32, (t_dev, t_dev), 1)
    earlier = jnp.where(row < col, 1.0, 0.0).astype(BF16)
    slot_of = jnp.dot(chosen.astype(BF16), earlier, preferred_element_type=F32)
    code_t = jnp.where(chosen > 0.5, slot_of, -1.0)
    scores = logits[...]
    powers = jnp.exp(scores - jnp.max(scores, axis=0, keepdims=True))
    probs_t = powers / jnp.sum(powers, axis=0, keepdims=True)
    PT[...] = probs_t
    gate_t = probs_t.astype(BF16).astype(F32)
    CS[...] = jnp.zeros_like(CS)
    GS[...] = jnp.zeros_like(GS)
    ACC[...] = jnp.zeros_like(ACC)
    for s in range(experts):
        CS[s, 0:1, :] = code_t[s : s + 1, :]
        CS[s, 1:2, :] = gate_t[s : s + 1, :]

    def send_code(k, carry):
        c_copy((e + k) % experts, e).start()
        return carry

    load_master.wait()
    stage0(0)
    lax.fori_loop(1, experts, send_code, 0)
    load_hidden.wait()
    HT[...] = hid[...].T

    def tick(i, carry):
        at_stage(i, 5 * HOP, stage_r1)
        at_stage(i, 6 * HOP, stage_r2)
        at_stage(i, 7 * HOP, stage_r3)
        at_stage(i, 8 * HOP, stage_r4)

        @pl.when(jnp.logical_and(i > 0, i < nc))
        def _():
            stage0(i)

        at_stage(i, HOP, stage1)
        at_stage(i, 2 * HOP, stage2)
        at_stage(i, 3 * HOP, stage3)
        at_stage(i, 4 * HOP, stage_c)
        return carry

    lax.fori_loop(0, nc + 8 * HOP, tick, 0)

    def wait_gain(k, carry):
        peer = (e + k) % experts
        g_copy(peer, peer).wait_recv()
        return carry

    lax.fori_loop(1, experts, wait_gain, 0)
    gain = jnp.concatenate([GR[s][0:1, :] for s in range(experts)], axis=0)
    probs_t = PT[...]
    router_out[...] = probs_t * (gain - jnp.sum(probs_t * gain, axis=0, keepdims=True))

    for kind in range(SIB_F + 2):
        left(ss.at[kind], G.at[:, kind])
    left(ss.at[WZ], W.at[:, 0, 0:2])
    left(ss.at[WZF], W.at[:, 0, 0])
    left(ss.at[WY], W.at[:, 0:2])
    left(ss.at[WYF], W.at[:, 0])
    left(ss.at[SF], S.at[:, 0])
    left(ss.at[SR], S.at[:, 0:2])
    for j in range(nc - KEEP, nc):
        release(j)

    def drain_small(k, carry):
        peer = (e + k) % experts
        c_copy(peer, e).wait_send()
        g_copy(peer, e).wait_send()
        return carry

    lax.fori_loop(1, experts, drain_small, 0)


def exchange(out_grad, logits, choices, saved, master):
    t_dev, width = out_grad.shape
    experts = logits.shape[0]
    rows_all, ff = saved.shape
    own = master.shape[0] * 128 // width
    nc = PARTS
    C = width // nc
    vm = pl.BlockSpec(memory_space=pltpu.VMEM)
    hbm = pl.BlockSpec(memory_space=pl.ANY)
    dma = pltpu.SemaphoreType.DMA
    return pl.pallas_call(
        kernel,
        out_shape=(
            jax.ShapeDtypeStruct(master.shape, F32),
            jax.ShapeDtypeStruct((experts, t_dev), F32),
        ),
        in_specs=[hbm, vm, vm, hbm, hbm],
        out_specs=(vm, vm),
        scratch_shapes=[
            pltpu.VMEM((nc, experts, t_dev, C), BF16),
            pltpu.VMEM((nc, NZ, NY, own, C), BF16),
            pltpu.VMEM((KEEP, NZ, NY, own, C), BF16),
            pltpu.VMEM((nc, 2, 2, own, C), BF16),
            pltpu.VMEM((nc, 2, NZ, own, C), BF16),
            pltpu.VMEM((nc, NZ, own, C), BF16),
            pltpu.VMEM((nc, 2, own, C // 2), BF16),
            pltpu.VMEM((nc, 2, own, C), BF16),
            pltpu.VMEM(saved.shape, BF16),
            pltpu.VMEM(master.shape, F32),
            pltpu.VMEM((ff, rows_all), BF16),
            pltpu.VMEM((experts // 2, 4 * (rows_all // experts), 2 * t_dev), BF16),
            pltpu.VMEM((rows_all, C), BF16),
            pltpu.VMEM((rows_all, C), BF16),
            pltpu.VMEM((rows_all, 128), F32),
            pltpu.VMEM((experts, 8, t_dev), F32),
            pltpu.VMEM((experts, 8, t_dev), F32),
            pltpu.VMEM((experts, 8, t_dev), F32),
            pltpu.VMEM((experts, 8, t_dev), F32),
            pltpu.VMEM((experts, t_dev), F32),
            dma((SENDS,)),
            dma((RECVS, nc)),
            dma((KEEP,)),
            dma((nc,)),
            dma((2,)),
            dma((experts,)),
            dma((experts,)),
            dma((experts,)),
            dma((experts,)),
        ],
        compiler_params=pltpu.CompilerParams(
            collective_id=0, has_side_effects=True, vmem_limit_bytes=62 * 1024 * 1024
        ),
    )(out_grad, choices, logits, saved, master)


def shards(out_grad, router_logits, choice_ids, hidden, master, first, second):
    saved = hidden.reshape(hidden.shape[2] * hidden.shape[3], hidden.shape[4])
    grad, router_grad = exchange(
        out_grad, router_logits.T, choice_ids.T, saved, master.reshape(-1, 128)
    )
    grad = grad.reshape(master.shape)
    new_first = beta_one * first + (1.0 - beta_one) * grad
    new_second = beta_two * second + (1.0 - beta_two) * grad * grad
    first_hat = new_first / (1.0 - beta_one**adam_step)
    second_hat = new_second / (1.0 - beta_two**adam_step)
    new_weight = master - learn_rate * (
        first_hat / (jnp.sqrt(second_hat) + epsilon) + decay_rate * master
    )
    return (new_weight, new_first, new_second, router_grad.T)


def solution(mesh):
    return jax.shard_map(
        shards,
        mesh=mesh,
        in_specs=(
            P(("dp", "expert"), None),
            P(("dp", "expert"), None),
            P(("dp", "expert"), None),
            P("dp", "expert", None, None, None),
            P("dp", "expert", None),
            P("dp", "expert", None),
            P("dp", "expert", None),
        ),
        out_specs=(
            P("dp", "expert", None),
            P("dp", "expert", None),
            P("dp", "expert", None),
            P(("dp", "expert"), None),
        ),
        check_vma=False,
    )
```

time: 200 us -> 177 us (0.89)
  the two profiles are of different devices: /device:TPU:48 before, /device:TPU:1 now
where the time goes in v2:
time: 177 us; the launch traced here: 175 us
  Pallas kernels  165 us (93%)
  other arithmetic  8.98 us (5%)
    pallas_call x1, Pallas kernels, exchange(): pl.pallas_call(kernel, out_shape=(jax.ShapeDtypeStruct(master.shape, F32)...  165 us
    sub x1, other arithmetic, shards(): master - learn_rate * (first_hat / (jnp.sqrt(second_hat) + epsilon) + dec...  8.98 us

profile of v2, /device:TPU:1, one launch (start us, length us, event | category | flops | bytes accessed | tf_op | source)
XLA Modules:
  0.0 175.2 jit_solution(8959428352907547050)
XLA Ops:
  0.6 0.0 copy-start
  0.6 0.0 copy-start.1
  0.7 164.9 %shard_map.102 = (f32[1920,128]{1,0:T(8,128)}, f32[16,128]{1,0:T(8,128)}) custom-call(bf16[128,5120]{1,0:T(8,128)(2,1)} %og.1, s32[6,128]{1,0:T(8,128)} %bitcast.11, f32[16,128]{1,0:T(8,128)} %bitcast.9, bf16[896,768]{1,0:T(8,128)(2,1)} %bitcast.7, f32[1920,128]{1,0:T(8,128)} %bitcast.6), custom_call_target="tpu_custom_call" | custom-call | tf_op jit(solution)/shard_map/pallas_call | solution.py:379
  165.6 0.0 copy-done
  165.6 0.0 copy-done.1
  165.6 0.0 copy-start.2
  165.6 9.0 %multiply_subtract_fusion = (f32[48,1,5120]{2,1,0:T(1,128)}, f32[48,1,5120]{2,1,0:T(1,128)}, f32[48,1,5120]{2,1,0:T(1,128)}) fusion(f32[48,1,5120]{2,1,0:T(1,128)S(1)} %copy-done, f32[48,1,5120]{2,1,0:T(1,128)} %bitcast.8, f32[48,1,5120]{2,1,0:T(1,128)S(1)} %copy-done.1, f32[48,1,5120]{2,1,0:T(1,128)} %param.13), kind=kLoop, calls=%fused_computation.2 | loop fusion | flops 3686400 | bytes 6881280 | tf_op jit(solution)/shard_map/sub | solution.py:434
  174.6 0.0 copy-done.2
  174.6 0.6 copy.15
Async XLA Ops:
  0.6 165.0 %copy-start = (f32[48,1,5120]{2,1,0:T(1,128)S(1)}, f32[48,1,5120]{2,1,0:T(1,128)}, u32[]{:S(2)}) copy-start(f32[48,1,5120]{2,1,0:T(1,128)} %param.11) | copy-start | bytes 2949124
  0.6 165.0 %copy-start.1 = (f32[48,1,5120]{2,1,0:T(1,128)S(1)}, f32[48,1,5120]{2,1,0:T(1,128)}, u32[]{:S(2)}) copy-start(f32[48,1,5120]{2,1,0:T(1,128)} %param.12) | copy-start | bytes 2949124
  165.6 9.0 %copy-start.2 = (f32[16,128]{1,0:T(8,128)S(1)}, f32[16,128]{1,0:T(8,128)}, u32[]{:S(2)}) copy-start(f32[16,128]{1,0:T(8,128)} %get-tuple-element.7) | copy-start | bytes 24580

commit v3 on v2

--- a/solution.py
+++ b/solution.py
@@ -22,6 +22,8 @@
 PARTS = 20
 HOP = 2
 KEEP = 2 * HOP + 2
+Y_FIRST = 5
+STRAIGHT = 3
 
 Z_OWN, XP_OWN, XM_OWN, SIB_OWN = 0, 1, 2, 3
 XP_PART, XM_PART, SIB_PART = 4, 5, 6
@@ -63,6 +65,7 @@
     zm = (did(down(z), y), e)
     yp = (did(z, up(y)), e)
     ym = (did(z, down(y)), e)
+    zo = (did(opp(z), y), e)
 
     def rc(send, recv, src, dst, dev):
         return pltpu.make_async_remote_copy(
@@ -135,6 +138,57 @@
         @pl.when(jnp.logical_and(j >= 0, j < nc))
         def _():
             fn(j)
+
+    def weights_by_order(j, send):
+        turned = j % Y_FIRST == Y_FIRST - 1
+
+        @pl.when(turned)
+        def _():
+            send(j, True)
+
+        @pl.when(jnp.logical_not(turned))
+        def _():
+            send(j, False)
+
+    def place(j, a, b, y_first):
+        return W.at[j, b, a] if y_first else W.at[j, a, b]
+
+    def weights0(j, y_first):
+        ref = W.at[j, z, y]
+        for dev in (yp, ym) if y_first else (zp, zm):
+            send_w(WZ, R_WZ, j, ref, dev)
+        for dev in (zp, zm) if y_first else (yp, ym):
+            send_w(WY, R_WY, j, ref, dev)
+
+    def weights1(j, y_first):
+        a, b = (y, z) if y_first else (z, y)
+        before, after = place(j, down(a), b, y_first), place(j, up(a), b, y_first)
+        ahead, back = (yp, ym) if y_first else (zp, zm)
+
+        @pl.when(j % 2 == 0)
+        def _():
+            send_w(WZF, R_WZF, j, before, ahead)
+
+        @pl.when(j % 2 == 1)
+        def _():
+            send_w(WZF, R_WZF, j, after, back)
+
+        for dev in (zp, zm) if y_first else (yp, ym):
+            send_w(WY, R_WY, j, before, dev)
+            send_w(WY, R_WY, j, after, dev)
+
+    def weights2(j, y_first):
+        a, b = (y, z) if y_first else (z, y)
+        for dev in (zp, zm) if y_first else (yp, ym):
+            send_w(WY, R_WY, j, place(j, opp(a), b, y_first), dev)
+
+    def weights3(j, y_first):
+        if y_first:
+            send_w(WYF, R_WYF, j, W.at[j, down(z), 0:2], zp)
+            send_w(WYF, R_WYF, j, W.at[j, up(z), 2:4], zm)
+        else:
+            send_w(WYF, R_WYF, j, W.at[j, 0:2, down(y)], yp)
+            send_w(WYF, R_WYF, j, W.at[j, 2:4, up(y)], ym)
 
     def stage0(j):
         local_g(j).wait()
@@ -144,8 +198,7 @@
         send_d(XP_OWN, R_X, j, zl, x, xp)
         send_d(XM_OWN, R_X, j, zl, x, xm)
         send_d(SIB_OWN, R_SIB, j, zl, x, sib)
-        send_w(WZ, R_WZ, j, W.at[j, z, y], zp)
-        send_w(WZ, R_WZ, j, W.at[j, z, y], zm)
+        weights_by_order(j, weights0)
 
     def stage1(j):
         arrive(R_Z, j, G.at[j, 0])
@@ -153,29 +206,20 @@
         send_d(XM_PART, R_X, j, 1 - zl, x, xm)
         send_d(SIB_PART, R_SIB, j, 1 - zl, x, sib)
         arrive(R_WZ, j, W.at[j, 0, 0:2])
-
-        @pl.when(j % 2 == 0)
-        def _():
-            send_w(WZF, R_WZF, j, W.at[j, down(z), y], zp)
-
-        @pl.when(j % 2 == 1)
-        def _():
-            send_w(WZF, R_WZF, j, W.at[j, up(z), y], zm)
+        weights_by_order(j, weights1)
 
     def stage2(j):
         arrive(R_X, j, G.at[j, 0:4])
         send_d(XP_FWD, R_XF, j, 0, down(x), xp)
         send_d(XM_FWD, R_XF, j, 1, up(x), xm)
         arrive(R_WZF, j, W.at[j, 0, 0])
-        send_w(WY, R_WY, j, W.at[j, :, y], yp)
-        send_w(WY, R_WY, j, W.at[j, :, y], ym)
+        weights_by_order(j, weights2)
         for k, (a, b) in enumerate(((0, down(x)), (1, down(x)), (0, up(x)), (1, up(x)))):
             send_d(SIB_X + k, R_SIB, j, a, b, sib)
 
     def stage3(j):
         arrive(R_WY, j, W.at[j, 0:2])
-        send_w(WYF, R_WYF, j, W.at[j, 0:2, down(y)], yp)
-        send_w(WYF, R_WYF, j, W.at[j, 2:4, up(y)], ym)
+        weights_by_order(j, weights3)
         arrive(R_XF, j, G.at[j, 0:2])
         for k in range(2):
             send_d(SIB_F + k, R_SIB, j, k, opp(x), sib)
@@ -271,19 +315,39 @@
         slot = pslot(j)
         arrive(R_RY, j, RY.at[j])
         S[j] = (PB[slot, :, y].astype(F32) + RY[j, 0].astype(F32) + RY[j, 1].astype(F32)).astype(BF16)
-        rc(ss.at[SF], rs.at[R_FZ, j], S.at[j, opp(z), :, 0:half], FZ.at[j, 0], zp).start()
-        rc(ss.at[SF], rs.at[R_FZ, j], S.at[j, opp(z), :, half:C], FZ.at[j, 1], zm).start()
+
+        @pl.when(j < nc - STRAIGHT)
+        def _():
+            rc(ss.at[SF], rs.at[R_FZ, j], S.at[j, opp(z), :, 0:half], FZ.at[j, 0], zp).start()
+            rc(ss.at[SF], rs.at[R_FZ, j], S.at[j, opp(z), :, half:C], FZ.at[j, 1], zm).start()
+
+        @pl.when(j >= nc - STRAIGHT)
+        def _():
+            rc(ss.at[SF], rs.at[R_RZ, j], S.at[j, opp(z)], RZ.at[j, 2], zo).start()
+            rc(ss.at[SR], rs.at[R_RZ, j], S.at[j, up(z)], RZ.at[j, 0], zp).start()
+            rc(ss.at[SR], rs.at[R_RZ, j], S.at[j, down(z)], RZ.at[j, 1], zm).start()
 
     def stage_r3(j):
-        arrive(R_FZ, j, FZ.at[j])
-        S[j, up(z), :, 0:half] = add(S[j, up(z), :, 0:half], FZ[j, 0])
-        rc(ss.at[SR], rs.at[R_RZ, j], S.at[j, up(z)], RZ.at[j, 0], zp).start()
-        S[j, down(z), :, half:C] = add(S[j, down(z), :, half:C], FZ[j, 1])
-        rc(ss.at[SR], rs.at[R_RZ, j], S.at[j, down(z)], RZ.at[j, 1], zm).start()
+        @pl.when(j < nc - STRAIGHT)
+        def _():
+            arrive(R_FZ, j, FZ.at[j])
+            S[j, up(z), :, 0:half] = add(S[j, up(z), :, 0:half], FZ[j, 0])
+            rc(ss.at[SR], rs.at[R_RZ, j], S.at[j, up(z)], RZ.at[j, 0], zp).start()
+            S[j, down(z), :, half:C] = add(S[j, down(z), :, half:C], FZ[j, 1])
+            rc(ss.at[SR], rs.at[R_RZ, j], S.at[j, down(z)], RZ.at[j, 1], zm).start()
 
     def stage_r4(j):
-        arrive(R_RZ, j, RZ.at[j])
-        total = S[j, z].astype(F32) + RZ[j, 0].astype(F32) + RZ[j, 1].astype(F32)
+        @pl.when(j < nc - STRAIGHT)
+        def _():
+            arrive(R_RZ, j, RZ.at[j, 0:2])
+            store(j, S[j, z].astype(F32) + RZ[j, 0].astype(F32) + RZ[j, 1].astype(F32))
+
+        @pl.when(j >= nc - STRAIGHT)
+        def _():
+            arrive(R_RZ, j, RZ.at[j])
+            store(j, S[j, z].astype(F32) + RZ[j, 0].astype(F32) + RZ[j, 1].astype(F32) + RZ[j, 2].astype(F32))
+
+    def store(j, total):
         for k in range(C // 128):
             grad_out[flat(j, k), :] = total[:, k * 128 : (k + 1) * 128]
 
@@ -319,6 +383,7 @@
     HT[...] = hid[...].T
 
     def tick(i, carry):
+        at_stage(i, 4 * HOP, stage_c)
         at_stage(i, 5 * HOP, stage_r1)
         at_stage(i, 6 * HOP, stage_r2)
         at_stage(i, 7 * HOP, stage_r3)
@@ -331,7 +396,6 @@
         at_stage(i, HOP, stage1)
         at_stage(i, 2 * HOP, stage2)
         at_stage(i, 3 * HOP, stage3)
-        at_stage(i, 4 * HOP, stage_c)
         return carry
 
     lax.fori_loop(0, nc + 8 * HOP, tick, 0)
@@ -392,7 +456,7 @@
             pltpu.VMEM((nc, 2, NZ, own, C), BF16),
             pltpu.VMEM((nc, NZ, own, C), BF16),
             pltpu.VMEM((nc, 2, own, C // 2), BF16),
-            pltpu.VMEM((nc, 2, own, C), BF16),
+            pltpu.VMEM((nc, 3, own, C), BF16),
             pltpu.VMEM(saved.shape, BF16),
             pltpu.VMEM(master.shape, F32),
             pltpu.VMEM((ff, rows_all), BF16),
@@ -423,10 +487,11 @@
 
 def shards(out_grad, router_logits, choice_ids, hidden, master, first, second):
     saved = hidden.reshape(hidden.shape[2] * hidden.shape[3], hidden.shape[4])
-    grad, router_grad = exchange(
-        out_grad, router_logits.T, choice_ids.T, saved, master.reshape(-1, 128)
+    shape = master.shape
+    master, first, second = lax.optimization_barrier(
+        tuple(v.reshape(-1, 128) for v in (master, first, second))
     )
-    grad = grad.reshape(master.shape)
+    grad, router_grad = exchange(out_grad, router_logits.T, choice_ids.T, saved, master)
     new_first = beta_one * first + (1.0 - beta_one) * grad
     new_second = beta_two * second + (1.0 - beta_two) * grad * grad
     first_hat = new_first / (1.0 - beta_one**adam_step)
@@ -434,7 +499,7 @@
     new_weight = master - learn_rate * (
         first_hat / (jnp.sqrt(second_hat) + epsilon) + decay_rate * master
     )
-    return (new_weight, new_first, new_second, router_grad.T)
+    return (*(v.reshape(shape) for v in (new_weight, new_first, new_second)), router_grad.T)
 
 
 def solution(mesh):

time: 177 us -> 155 us (0.88)
  Pallas kernels: 165 us -> 148 us
  other arithmetic: 8.98 us -> 3.55 us
    pallas_call x1, Pallas kernels: 165 us -> 148 us  [exchange(): pl.pallas_call(kernel, out_shape=(jax.ShapeDtypeStruct(master.shape, F32)...]
    sub x1, other arithmetic: 8.98 us -> 3.55 us  [shards(): master - learn_rate * (first_hat / (jnp.sqrt(second_hat) + epsilon) + dec...]
where the time goes in v3:
time: 155 us; the launch traced here: 153 us
  Pallas kernels  148 us (95%)
  other arithmetic  3.55 us (2%)
    pallas_call x1, Pallas kernels, exchange(): pl.pallas_call(kernel, out_shape=(jax.ShapeDtypeStruct(master.shape, F32)...  148 us
    sub x1, other arithmetic, shards(): master - learn_rate * (first_hat / (jnp.sqrt(second_hat) + epsilon) + dec...  3.55 us

profile of v3, /device:TPU:1, one launch (start us, length us, event | category | flops | bytes accessed | tf_op | source)
XLA Modules:
  0.0 153.2 jit_solution(2058615046593415569)
XLA Ops:
  0.6 0.0 copy-start
  0.6 0.0 copy-start.1
  0.7 148.4 %shard_map.102 = (f32[1920,128]{1,0:T(8,128)}, f32[16,128]{1,0:T(8,128)}) custom-call(bf16[128,5120]{1,0:T(8,128)(2,1)} %og.1, s32[6,128]{1,0:T(8,128)} %bitcast.20, f32[16,128]{1,0:T(8,128)} %bitcast.18, bf16[896,768]{1,0:T(8,128)(2,1)} %bitcast.12, f32[1920,128]{1,0:T(8,128)} %bitcast.10), custom_call_target="tpu_custom_call" | custom-call | tf_op jit(solution)/shard_map/pallas_call | solution.py:443
  149.0 0.0 copy-done
  149.0 0.0 copy-done.1
  149.0 0.0 copy-start.2
  149.0 3.5 %multiply_subtract_fusion = (f32[1920,128]{1,0:T(8,128)}, f32[1920,128]{1,0:T(8,128)}, f32[1920,128]{1,0:T(8,128)}) fusion(f32[1920,128]{1,0:T(8,128)S(1)} %bitcast.11, f32[1920,128]{1,0:T(8,128)} %get-tuple-element.11, f32[1920,128]{1,0:T(8,128)S(1)} %bitcast.13, f32[1920,128]{1,0:T(8,128)} %bitcast.14), kind=kLoop, calls=%fused_computation.2 | loop fusion | flops 3686400 | bytes 6881280 | tf_op jit(solution)/shard_map/sub | solution.py:499
  152.6 0.0 copy-done.2
  152.6 0.6 copy.15
Async XLA Ops:
  0.6 148.4 %copy-start = (f32[48,1,5120]{2,1,0:T(1,128)S(1)}, f32[48,1,5120]{2,1,0:T(1,128)}, u32[]{:S(2)}) copy-start(f32[48,1,5120]{2,1,0:T(1,128)} %param.11) | copy-start | bytes 2949124
  0.6 148.4 %copy-start.1 = (f32[48,1,5120]{2,1,0:T(1,128)S(1)}, f32[48,1,5120]{2,1,0:T(1,128)}, u32[]{:S(2)}) copy-start(f32[48,1,5120]{2,1,0:T(1,128)} %param.12) | copy-start | bytes 2949124
  149.0 3.6 %copy-start.2 = (f32[16,128]{1,0:T(8,128)S(1)}, f32[16,128]{1,0:T(8,128)}, u32[]{:S(2)}) copy-start(f32[16,128]{1,0:T(8,128)} %get-tuple-element.13) | copy-start | bytes 24580

commit v4 on v2

v4 whole, which is shorter than its diff:
```python
import functools

import jax
import jax.numpy as jnp
from jax import lax
from jax.experimental import pallas as pl
from jax.experimental.pallas import tpu as pltpu
from jax.sharding import PartitionSpec as P

beta_one = 0.9
beta_two = 0.95
learn_rate = 0.001
decay_rate = 0.1
epsilon = 1e-08
adam_step = 100.0

MESH = pl.DeviceIdType.MESH
F32 = jnp.float32
BF16 = jnp.bfloat16

NZ, NY, NX = 4, 4, 4
C = 128
AHEAD = 2
LAG_D = (0, 2, 4, 6)
LAG_S = (2, 4, 6)
FIRST = 10
SINGLE = 2
STRAIGHT = 2
T_W, T_CODE, T_H1 = 1, 3, 8
LAG_W = (1, 4)

Z_OWN, XP_OWN, XM_OWN, SIB_OWN = 0, 1, 2, 3
XP_PART, XM_PART, SIB_PART = 4, 5, 6
XP_FWD, XM_FWD = 7, 8
SIB_X = 9
SIB_F = 13
SA, SW, SWZ, SWF, SH, SHF, SF, SR, SY, SC, SG = range(15, 26)
SENDS = 26

(R_A, R_Z, R_X, R_XF, R_SIB, R_WZ, R_WF, R_FZ, R_RZ, R_RY) = range(10)
RECVS = 10
(O_W, O_H, O_HF, O_C, O_G) = range(5)
ONCE = 5


def kernel(
    og_in, ids, logits, hid_in, master_in, grad_out, router_out,
    G, W, WL, PB, FZ, RZ, S, RY, OG, HB, HT, master, OH, ROWS, SCALED, ACC, CS, CR, GP, GQ, GS, GR, PT,
    ss, rs, os_, l2, cs_s, cs_r, gs_s, gs_r,
):
    nc, experts, _, t_dev, _ = G.shape
    rows, ff = HB.shape[1:]
    cap = rows // experts
    d = lax.axis_index("dp")
    e = lax.axis_index("expert")
    z, y = d // NY, d % NY
    zl, x, core = e // (2 * NX), (e // 2) % NX, e % 2
    up = lambda v: (v + 1) % 4
    down = lambda v: (v + 3) % 4
    opp = lambda v: (v + 2) % 4
    eid = lambda a, b, c: a * (2 * NX) + b * 2 + c
    did = lambda a, b: a * NY + b

    part = (d, eid(1 - zl, x, core))
    xp = (d, eid(zl, up(x), core))
    xm = (d, eid(zl, down(x), core))
    sib = (d, eid(zl, x, 1 - core))
    zp = (did(up(z), y), e)
    zm = (did(down(z), y), e)
    zo = (did(opp(z), y), e)
    yp = (did(z, up(y)), e)
    ym = (did(z, down(y)), e)
    yo = (did(z, opp(y)), e)
    along_y = ((up(y), yp), (down(y), ym), (opp(y), yo))

    def rc(send, recv, src, dst, dev):
        return pltpu.make_async_remote_copy(
            src_ref=src, dst_ref=dst, send_sem=send, recv_sem=recv, device_id=dev, device_id_type=MESH
        )

    def arrive(recv, j, ref):
        rc(ss.at[0], rs.at[recv, j], ref, ref, sib).wait_recv()

    def arrive_once(recv, ref):
        rc(ss.at[0], os_.at[recv], ref, ref, sib).wait_recv()

    def left(send, ref):
        rc(ss.at[send], rs.at[0, 0], ref, ref, sib).wait_send()

    own, lanes_of = W.shape[3], NY * nc

    def flat(yy, j):
        return pl.ds(yy * nc + j, own, stride=lanes_of)

    def columns(yy, j):
        return pl.ds(pl.multiple_of((yy * nc + j) * C, C), C)

    load_tokens = pltpu.make_async_copy(og_in, OG, l2.at[0])
    load_master = pltpu.make_async_copy(master_in, master, l2.at[1])
    load_hidden = pltpu.make_async_copy(hid_in, HB.at[y], l2.at[2])
    load_tokens.start()
    load_master.start()
    load_hidden.start()

    barrier = pltpu.get_barrier_semaphore()

    def greet(k, carry):
        pl.semaphore_signal(barrier, inc=1, device_id=(d, (e + k) % experts), device_id_type=MESH)
        return carry

    lax.fori_loop(1, experts, greet, 0)
    for dev in (zp, zm, zo, yp, ym, yo):
        pl.semaphore_signal(barrier, inc=1, device_id=dev, device_id_type=MESH)
    pl.semaphore_wait(barrier, experts - 1 + 6)

    def send_d(kind, recv, j, a, b, dev):
        ref = G.at[j, eid(a, b, core)]
        rc(ss.at[kind], rs.at[recv, j], ref, ref, dev).start()

    def c_copy(peer, source):
        return pltpu.make_async_remote_copy(
            src_ref=CS.at[peer], dst_ref=CR.at[y, source], send_sem=cs_s.at[peer], recv_sem=cs_r.at[source],
            device_id=(d, peer), device_id_type=MESH,
        )

    def g_copy(peer, source):
        return pltpu.make_async_remote_copy(
            src_ref=GS.at[peer], dst_ref=GR.at[source], send_sem=gs_s.at[peer], recv_sem=gs_r.at[source],
            device_id=(d, peer), device_id_type=MESH,
        )

    def share_tokens(j, carry):
        for yy, dev in along_y:
            rc(ss.at[SA], rs.at[R_A, j], OG.at[:, columns(yy, j)], G.at[j, e, y], dev).start()
        G[j, e, y] = OG[:, columns(y, j)]
        return carry

    def tokens0(j):
        arrive(R_A, j, G.at[j, 0, 0:3])
        send_d(Z_OWN, R_Z, j, zl, x, part)
        send_d(XP_OWN, R_X, j, zl, x, xp)
        send_d(XM_OWN, R_X, j, zl, x, xm)
        send_d(SIB_OWN, R_SIB, j, zl, x, sib)

    def tokens1(j):
        arrive(R_Z, j, G.at[j, 0])
        send_d(XP_PART, R_X, j, 1 - zl, x, xp)
        send_d(XM_PART, R_X, j, 1 - zl, x, xm)
        send_d(SIB_PART, R_SIB, j, 1 - zl, x, sib)

    def tokens2(j):
        arrive(R_X, j, G.at[j, 0:4])
        send_d(XP_FWD, R_XF, j, 0, down(x), xp)
        send_d(XM_FWD, R_XF, j, 1, up(x), xm)
        for k, (a, b) in enumerate(((0, down(x)), (1, down(x)), (0, up(x)), (1, up(x)))):
            send_d(SIB_X + k, R_SIB, j, a, b, sib)

    def tokens3(j):
        arrive(R_XF, j, G.at[j, 0:2])
        for k in range(2):
            send_d(SIB_F + k, R_SIB, j, k, opp(x), sib)

    def share_weights():
        def cast(j, carry):
            for yy in range(NY):
                WL[yy, j] = master[flat(yy, j), :].astype(BF16)
            return carry

        lax.fori_loop(0, nc, cast, 0)
        for yy, dev in along_y:
            rc(ss.at[SW], os_.at[O_W], WL.at[yy], W.at[z, y], dev).start()
        W[z, y] = WL[y]

    def weights1(j):
        rc(ss.at[SWZ], rs.at[R_WZ, j], W.at[z, :, j], W.at[z, :, j], zp).start()
        rc(ss.at[SWZ], rs.at[R_WZ, j], W.at[z, :, j], W.at[z, :, j], zm).start()

    def weights2(j):
        arrive(R_WZ, j, W.at[0:2, :, j])
        before, after = W.at[down(z), 0:2, j], W.at[up(z), 2:4, j]
        rc(ss.at[SWF], rs.at[R_WF, j], before, before, zp).start()
        rc(ss.at[SWF], rs.at[R_WF, j], after, after, zm).start()

    def share_hidden():
        load_hidden.wait()
        rc(ss.at[SH], os_.at[O_H], HB.at[y], HB.at[y], yp).start()
        rc(ss.at[SH], os_.at[O_H], HB.at[y], HB.at[y], ym).start()

    def hidden1():
        arrive_once(O_H, HB.at[0:2])
        before, after = HB.at[down(y), 0 : rows // 2], HB.at[up(y), rows // 2 : rows]
        rc(ss.at[SHF], os_.at[O_HF], before, before, yp).start()
        rc(ss.at[SHF], os_.at[O_HF], after, after, ym).start()

    def codes1():
        def wait_code(k, carry):
            peer = (e + k) % experts
            c_copy(peer, peer).wait_recv()
            return carry

        lax.fori_loop(1, experts, wait_code, 0)
        CR[y, pl.ds(e, 1)] = CS[pl.ds(e, 1)]
        for _, dev in along_y:
            rc(ss.at[SC], os_.at[O_C], CR.at[y], CR.at[y], dev).start()

    def setup():
        arrive_once(O_C, CR.at[0:3])
        slots = lax.broadcasted_iota(jnp.int32, (cap, t_dev), 0).astype(F32)
        empty = jnp.zeros((cap, t_dev), F32)

        def select(yy, carry):
            for p in range(experts // 2):
                one, weighted = [], []
                for s in range(2):
                    tile = CR[yy, 2 * p + s]
                    hot = jnp.where(slots == tile[0:1, :], 1.0, 0.0)
                    gate = hot * tile[1:2, :]
                    one.append(jnp.concatenate([hot, empty] if s == 0 else [empty, hot], axis=1))
                    weighted.append(jnp.concatenate([gate, empty] if s == 0 else [empty, gate], axis=1))
                OH[yy, p] = jnp.concatenate(one + weighted, axis=0).astype(BF16)
            return carry

        lax.fori_loop(0, NY, select, 0)

    def setup_hidden():
        arrive_once(O_HF, HB.at[0])
        for yy in range(NY):
            HT[:, yy * rows : (yy + 1) * rows] = HB[yy].T

    def matmuls(j, n):
        for k in range(n):
            arrive(R_SIB, j + k, G.at[j + k, 0:8])
        pair = 2 * cap
        width = n * C

        def side(parts):
            return parts[0] if n == 1 else jnp.concatenate(parts, axis=1)

        def select(yy, carry):
            for p in range(experts // 2):
                tokens = side([G[j + k, 2 * p : 2 * p + 2, yy].reshape(2 * t_dev, C) for k in range(n)])
                picked = jnp.dot(OH[yy, p], tokens, preferred_element_type=F32)
                at = pl.ds(pl.multiple_of(yy * rows + p * pair, 16), pair)
                ROWS[at, 0:width] = picked[:pair].astype(BF16)
                SCALED[at, 0:width] = picked[pair:].astype(BF16)
            return carry

        lax.fori_loop(0, NY, select, 0)
        partial = jnp.dot(HT[...], SCALED[:, 0:width], preferred_element_type=F32).astype(BF16)
        for k in range(n):
            PB[j + k] = partial[:, k * C : (k + 1) * C].reshape(NZ, NY, own, C)
            send_sums(j + k)

        for k in range(n):
            arrive(R_WF, j + k, W.at[0, :, j + k])
        weights = side([W[:, :, j + k].reshape(ff, C) for k in range(n)])

        def through(yy, carry):
            at = pl.ds(pl.multiple_of(yy * rows, rows), rows)
            product = jnp.dot(HB[yy], weights, preferred_element_type=F32) * ROWS[at, 0:width].astype(F32)
            total = product[:, 0:C]
            for k in range(1, n):
                total = total + product[:, k * C : (k + 1) * C]
            ACC[at, :] += total
            return carry

        lax.fori_loop(0, NY, through, 0)

    def send_sums(j):
        @pl.when(j < nc - STRAIGHT)
        def _():
            rc(ss.at[SF], rs.at[R_FZ, j], PB.at[j, opp(z), 2:4], FZ.at[j, 0], zp).start()
            rc(ss.at[SF], rs.at[R_FZ, j], PB.at[j, opp(z), 0:2], FZ.at[j, 1], zm).start()

        @pl.when(j >= nc - STRAIGHT)
        def _():
            rc(ss.at[SF], rs.at[R_RZ, j], PB.at[j, opp(z)], RZ.at[j, 2], zo).start()
            rc(ss.at[SR], rs.at[R_RZ, j], PB.at[j, up(z)], RZ.at[j, 0], zp).start()
            rc(ss.at[SR], rs.at[R_RZ, j], PB.at[j, down(z)], RZ.at[j, 1], zm).start()

    def add(a, b):
        return (a.astype(F32) + b.astype(F32)).astype(BF16)

    def sums1(j):
        @pl.when(j < nc - STRAIGHT)
        def _():
            arrive(R_FZ, j, FZ.at[j])
            PB[j, up(z), 2:4] = add(PB[j, up(z), 2:4], FZ[j, 0])
            rc(ss.at[SR], rs.at[R_RZ, j], PB.at[j, up(z)], RZ.at[j, 0], zp).start()
            PB[j, down(z), 0:2] = add(PB[j, down(z), 0:2], FZ[j, 1])
            rc(ss.at[SR], rs.at[R_RZ, j], PB.at[j, down(z)], RZ.at[j, 1], zm).start()

    def sums2(j):
        @pl.when(j < nc - STRAIGHT)
        def _():
            arrive(R_RZ, j, RZ.at[j, 0:2])
            S[j] = PB[j, z].astype(F32) + RZ[j, 0].astype(F32) + RZ[j, 1].astype(F32)

        @pl.when(j >= nc - STRAIGHT)
        def _():
            arrive(R_RZ, j, RZ.at[j])
            S[j] = PB[j, z].astype(F32) + RZ[j, 0].astype(F32) + RZ[j, 1].astype(F32) + RZ[j, 2].astype(F32)

        for yy, dev in along_y:
            rc(ss.at[SY], rs.at[R_RY, j], S.at[j, yy], RY.at[j, y], dev).start()

    def sums3(j):
        arrive(R_RY, j, RY.at[j, 0:3])
        RY[j, y] = S[j, y]
        for yy in range(NY):
            grad_out[flat(yy, j), :] = RY[j, yy]

    def send_scores():
        slots = lax.broadcasted_iota(jnp.int32, (cap, t_dev), 0).astype(F32)

        def one(yy, carry):
            score = jnp.sum(ACC[pl.ds(pl.multiple_of(yy * rows, rows), rows), :], axis=1, keepdims=True)
            for s in range(experts):
                hot = slots == CR[yy, s][0:1, :]
                GP[yy, s : s + 1, :] = jnp.sum(
                    jnp.where(hot, score[s * cap : (s + 1) * cap, :], 0.0), axis=0, keepdims=True
                )
            return carry

        lax.fori_loop(0, NY, one, 0)
        for yy, dev in along_y:
            rc(ss.at[SG], os_.at[O_G], GP.at[yy], GQ.at[y], dev).start()

    def send_gains():
        arrive_once(O_G, GQ.at[0:3])
        GQ[y] = GP[y]
        total = GQ[0] + GQ[1] + GQ[2] + GQ[3]
        for s in range(experts):
            GS[s, 0:1, :] = total[s : s + 1, :]

        def send(k, carry):
            g_copy((e + k) % experts, e).start()
            return carry

        lax.fori_loop(1, experts, send, 0)
        GR[pl.ds(e, 1)] = GS[pl.ds(e, 1)]

    load_tokens.wait()
    lax.fori_loop(0, nc, share_tokens, 0)

    labels = lax.broadcasted_iota(jnp.int32, (experts, t_dev), 0)
    chosen = jnp.zeros((experts, t_dev), F32)
    for k in range(ids.shape[0]):
        chosen = chosen + jnp.where(ids[k : k + 1, :] == labels, 1.0, 0.0)
    row = lax.broadcasted_iota(jnp.int32, (t_dev, t_dev), 0)
    col = lax.broadcasted_iota(jnp.int32, (t_dev, t_dev), 1)
    earlier = jnp.where(row < col, 1.0, 0.0).astype(BF16)
    slot_of = jnp.dot(chosen.astype(BF16), earlier, preferred_element_type=F32)
    code_t = jnp.where(chosen > 0.5, slot_of, -1.0)
    scores = logits[...]
    powers = jnp.exp(scores - jnp.max(scores, axis=0, keepdims=True))
    probs_t = powers / jnp.sum(powers, axis=0, keepdims=True)
    PT[...] = probs_t
    gate_t = probs_t.astype(BF16).astype(F32)
    CS[...] = jnp.zeros_like(CS)
    GS[...] = jnp.zeros_like(GS)
    ACC[...] = jnp.zeros_like(ACC)
    for s in range(experts):
        CS[s, 0:1, :] = code_t[s : s + 1, :]
        CS[s, 1:2, :] = gate_t[s : s + 1, :]

    def send_code(k, carry):
        c_copy((e + k) % experts, e).start()
        return carry

    lax.fori_loop(1, experts, send_code, 0)
    load_master.wait()
    share_weights()
    share_hidden()

    doubles = (nc - SINGLE) // 2
    last = FIRST + doubles + SINGLE - 1

    def after_matmuls(i, lag, fn):
        u = i - FIRST - lag

        @pl.when(jnp.logical_and(u >= 0, u < doubles))
        def _():
            fn(2 * u)
            fn(2 * u + 1)

        @pl.when(jnp.logical_and(u >= doubles, u < doubles + SINGLE))
        def _():
            fn(u + doubles)

    def once(i, tick, fn):
        @pl.when(i == tick)
        def _():
            fn()

    def tick(i, carry):
        def first_tokens(j, carry):
            tokens0(j)
            return carry

        begin, end = jnp.where(i == 0, 0, jnp.minimum(i + AHEAD, nc)), jnp.minimum(i + AHEAD + 1, nc)
        lax.fori_loop(begin, end, first_tokens, 0)

        for lag, stage in zip(LAG_D[1:], (tokens1, tokens2, tokens3)):
            j = i - lag

            @pl.when(jnp.logical_and(j >= 0, j < nc))
            def _():
                stage(j)

        @pl.when(i == T_W)
        def _():
            arrive_once(O_W, W.at[0, 0:3])

        for lag, stage in zip(LAG_W, (weights1, weights2)):
            j = i - lag

            @pl.when(jnp.logical_and(j >= 0, j < nc))
            def _():
                stage(j)

        once(i, T_CODE, codes1)
        once(i, T_H1, hidden1)
        once(i, FIRST - 1, setup)
        once(i, FIRST, setup_hidden)
        after_matmuls(i, LAG_S[0], sums1)
        after_matmuls(i, LAG_S[1], sums2)
        u = i - FIRST

        @pl.when(jnp.logical_and(u >= 0, u < doubles))
        def _():
            matmuls(2 * u, 2)

        @pl.when(jnp.logical_and(u >= doubles, u < doubles + SINGLE))
        def _():
            matmuls(u + doubles, 1)

        once(i, last, send_scores)
        once(i, last + 2, send_gains)
        after_matmuls(i, LAG_S[2], sums3)
        return carry

    lax.fori_loop(0, last + LAG_S[2] + 1, tick, 0)

    def wait_gain(k, carry):
        peer = (e + k) % experts
        g_copy(peer, peer).wait_recv()
        return carry

    lax.fori_loop(1, experts, wait_gain, 0)
    gain = jnp.concatenate([GR[s][0:1, :] for s in range(experts)], axis=0)
    probs_t = PT[...]
    router_out[...] = probs_t * (gain - jnp.sum(probs_t * gain, axis=0, keepdims=True))

    left(SA, G.at[:, 0, 0:3])
    for kind in range(SIB_F + 2):
        left(kind, G.at[:, kind])
    left(SW, W.at[0, 0:3])
    left(SWZ, W.at[0:2])
    left(SWF, W.at[0])
    left(SH, HB.at[0:2])
    left(SHF, HB.at[0])
    left(SF, PB.at[:, 0])
    left(SR, PB.at[:, 0:2])
    left(SY, S.at[:, 0:3])
    left(SC, CR.at[0:3])
    left(SG, GP.at[0:3])

    def drain_small(k, carry):
        peer = (e + k) % experts
        c_copy(peer, e).wait_send()
        g_copy(peer, e).wait_send()
        return carry

    lax.fori_loop(1, experts, drain_small, 0)


def exchange(out_grad, logits, choices, saved, master):
    t_dev, width = out_grad.shape
    experts = logits.shape[0]
    rows, ff = saved.shape
    own = master.shape[0] * 128 // width
    nc = width // (NY * C)
    cap = rows // experts
    vm = pl.BlockSpec(memory_space=pltpu.VMEM)
    hbm = pl.BlockSpec(memory_space=pl.ANY)
    dma = pltpu.SemaphoreType.DMA
    return pl.pallas_call(
        kernel,
        out_shape=(
            jax.ShapeDtypeStruct(master.shape, F32),
            jax.ShapeDtypeStruct((experts, t_dev), F32),
        ),
        in_specs=[hbm, vm, vm, hbm, hbm],
        out_specs=(vm, vm),
        scratch_shapes=[
            pltpu.VMEM((nc, experts, NY, t_dev, C), BF16),
            pltpu.VMEM((NZ, NY, nc, own, C), BF16),
            pltpu.VMEM((NY, nc, own, C), BF16),
            pltpu.VMEM((nc, NZ, NY, own, C), BF16),
            pltpu.VMEM((nc, 2, 2, own, C), BF16),
            pltpu.VMEM((nc, 3, NY, own, C), BF16),
            pltpu.VMEM((nc, NY, own, C), F32),
            pltpu.VMEM((nc, NY, own, C), F32),
            pltpu.VMEM((t_dev, width), BF16),
            pltpu.VMEM((NY, rows, ff), BF16),
            pltpu.VMEM((ff, NY * rows), BF16),
            pltpu.VMEM(master.shape, F32),
            pltpu.VMEM((NY, experts // 2, 4 * cap, 2 * t_dev), BF16),
            pltpu.VMEM((NY * rows, 2 * C), BF16),
            pltpu.VMEM((NY * rows, 2 * C), BF16),
            pltpu.VMEM((NY * rows, C), F32),
            pltpu.VMEM((experts, 8, t_dev), F32),
            pltpu.VMEM((NY, experts, 8, t_dev), F32),
            pltpu.VMEM((NY, experts, t_dev), F32),
            pltpu.VMEM((NY, experts, t_dev), F32),
            pltpu.VMEM((experts, 8, t_dev), F32),
            pltpu.VMEM((experts, 8, t_dev), F32),
            pltpu.VMEM((experts, t_dev), F32),
            dma((SENDS,)),
            dma((RECVS, nc)),
            dma((ONCE,)),
            dma((3,)),
            dma((experts,)),
            dma((experts,)),
            dma((experts,)),
            dma((experts,)),
        ],
        compiler_params=pltpu.CompilerParams(
            collective_id=0, has_side_effects=True, vmem_limit_bytes=62 * 1024 * 1024
        ),
    )(out_grad, choices, logits, saved, master)


def shards(out_grad, router_logits, choice_ids, hidden, master, first, second):
    saved = hidden.reshape(hidden.shape[2] * hidden.shape[3], hidden.shape[4])
    shape = master.shape
    master, first, second = lax.optimization_barrier(
        tuple(v.reshape(-1, 128) for v in (master, first, second))
    )
    grad, router_grad = exchange(out_grad, router_logits.T, choice_ids.T, saved, master)
    new_first = beta_one * first + (1.0 - beta_one) * grad
    new_second = beta_two * second + (1.0 - beta_two) * grad * grad
    first_hat = new_first / (1.0 - beta_one**adam_step)
    second_hat = new_second / (1.0 - beta_two**adam_step)
    new_weight = master - learn_rate * (
        first_hat / (jnp.sqrt(second_hat) + epsilon) + decay_rate * master
    )
    return (*(v.reshape(shape) for v in (new_weight, new_first, new_second)), router_grad.T)


def solution(mesh):
    return jax.shard_map(
        shards,
        mesh=mesh,
        in_specs=(
            P(("dp", "expert"), None),
            P(("dp", "expert"), None),
            P(("dp", "expert"), None),
            P("dp", "expert", None, None, None),
            P("dp", "expert", None),
            P("dp", "expert", None),
            P("dp", "expert", None),
        ),
        out_specs=(
            P("dp", "expert", None),
            P("dp", "expert", None),
            P("dp", "expert", None),
            P(("dp", "expert"), None),
        ),
        check_vma=False,
    )
```

time: 177 us -> 145 us (0.82); the launches traced: 175 us -> 145 us
  Pallas kernels: 165 us -> 140 us
  other arithmetic: 8.98 us -> 3.55 us
    pallas_call x1, Pallas kernels: 165 us -> 140 us  [exchange(): pl.pallas_call(kernel, out_shape=(jax.ShapeDtypeStruct(master.shape, F32)...]
    sub x1, other arithmetic: 8.98 us -> 3.55 us  [shards(): master - learn_rate * (first_hat / (jnp.sqrt(second_hat) + epsilon) + dec...]
where the time goes in v4:
time: 145 us
  Pallas kernels  140 us (97%)
  other arithmetic  3.55 us (2%)
    pallas_call x1, Pallas kernels, exchange(): pl.pallas_call(kernel, out_shape=(jax.ShapeDtypeStruct(master.shape, F32)...  140 us
    sub x1, other arithmetic, shards(): master - learn_rate * (first_hat / (jnp.sqrt(second_hat) + epsilon) + dec...  3.55 us

profile of v4, /device:TPU:1, one launch (start us, length us, event | category | flops | bytes accessed | tf_op | source)
XLA Modules:
  0.0 145.3 jit_solution(5219671252768236377)
XLA Ops:
  0.6 0.0 copy-start
  0.6 0.0 copy-start.1
  0.7 140.4 %shard_map.102 = (f32[1920,128]{1,0:T(8,128)}, f32[16,128]{1,0:T(8,128)}) custom-call(bf16[128,5120]{1,0:T(8,128)(2,1)} %og_in.1, s32[6,128]{1,0:T(8,128)} %bitcast.20, f32[16,128]{1,0:T(8,128)} %bitcast.18, bf16[896,768]{1,0:T(8,128)(2,1)} %bitcast.12, f32[1920,128]{1,0:T(8,128)} %bitcast.10), custom_call_target="tpu_custom_call" | custom-call | tf_op jit(solution)/shard_map/pallas_call | solution.py:488
  141.1 0.0 copy-done
  141.1 0.0 copy-done.1
  141.1 0.0 copy-start.2
  141.1 3.5 %multiply_subtract_fusion = (f32[1920,128]{1,0:T(8,128)}, f32[1920,128]{1,0:T(8,128)}, f32[1920,128]{1,0:T(8,128)}) fusion(f32[1920,128]{1,0:T(8,128)S(1)} %bitcast.11, f32[1920,128]{1,0:T(8,128)} %get-tuple-element.11, f32[1920,128]{1,0:T(8,128)S(1)} %bitcast.13, f32[1920,128]{1,0:T(8,128)} %bitcast.14), kind=kLoop, calls=%fused_computation.2 | loop fusion | flops 3686400 | bytes 6881280 | tf_op jit(solution)/shard_map/sub | solution.py:546
  144.7 0.0 copy-done.2
  144.7 0.6 copy.15
Async XLA Ops:
  0.6 140.5 %copy-start = (f32[48,1,5120]{2,1,0:T(1,128)S(1)}, f32[48,1,5120]{2,1,0:T(1,128)}, u32[]{:S(2)}) copy-start(f32[48,1,5120]{2,1,0:T(1,128)} %param.11) | copy-start | bytes 2949124
  0.6 140.5 %copy-start.1 = (f32[48,1,5120]{2,1,0:T(1,128)S(1)}, f32[48,1,5120]{2,1,0:T(1,128)}, u32[]{:S(2)}) copy-start(f32[48,1,5120]{2,1,0:T(1,128)} %param.12) | copy-start | bytes 2949124
  141.1 3.6 %copy-start.2 = (f32[16,128]{1,0:T(8,128)S(1)}, f32[16,128]{1,0:T(8,128)}, u32[]{:S(2)}) copy-start(f32[16,128]{1,0:T(8,128)} %get-tuple-element.13) | copy-start | bytes 24580

commit v5 on v4

--- a/solution.py
+++ b/solution.py
@@ -20,14 +20,14 @@
 
 NZ, NY, NX = 4, 4, 4
 C = 128
-AHEAD = 2
-LAG_D = (0, 2, 4, 6)
+AHEAD = 3
+LAG_D = (0, 1, 3, 5)
 LAG_S = (2, 4, 6)
-FIRST = 10
+FIRST = 9
 SINGLE = 2
 STRAIGHT = 2
-T_W, T_CODE, T_H1 = 1, 3, 8
-LAG_W = (1, 4)
+T_W, T_CODE, T_H1 = 1, 3, 7
+LAG_W = (1, 3)
 
 Z_OWN, XP_OWN, XM_OWN, SIB_OWN = 0, 1, 2, 3
 XP_PART, XM_PART, SIB_PART = 4, 5, 6

time: 145 us -> 139 us (0.959)
  Pallas kernels: 140 us -> 134 us
    pallas_call x1, Pallas kernels: 140 us -> 134 us  [exchange(): pl.pallas_call(kernel, out_shape=(jax.ShapeDtypeStruct(master.shape, F32)...]
where the time goes in v5:
time: 139 us
  Pallas kernels  134 us (96%)
  other arithmetic  3.55 us (3%)
    pallas_call x1, Pallas kernels, exchange(): pl.pallas_call(kernel, out_shape=(jax.ShapeDtypeStruct(master.shape, F32)...  134 us
    sub x1, other arithmetic, shards(): master - learn_rate * (first_hat / (jnp.sqrt(second_hat) + epsilon) + dec...  3.55 us

profile of v5, /device:TPU:1, one launch (start us, length us, event | category | flops | bytes accessed | tf_op | source)
XLA Modules:
  0.0 139.3 jit_solution(13619346453234597405)
XLA Ops:
  0.6 0.0 copy-start
  0.6 0.0 copy-start.1
  0.7 134.4 %shard_map.102 = (f32[1920,128]{1,0:T(8,128)}, f32[16,128]{1,0:T(8,128)}) custom-call(bf16[128,5120]{1,0:T(8,128)(2,1)} %og_in.1, s32[6,128]{1,0:T(8,128)} %bitcast.20, f32[16,128]{1,0:T(8,128)} %bitcast.18, bf16[896,768]{1,0:T(8,128)(2,1)} %bitcast.12, f32[1920,128]{1,0:T(8,128)} %bitcast.10), custom_call_target="tpu_custom_call" | custom-call | tf_op jit(solution)/shard_map/pallas_call | solution.py:488
  135.1 0.0 copy-done
  135.1 0.0 copy-done.1
  135.1 0.0 copy-start.2
  135.1 3.5 %multiply_subtract_fusion = (f32[1920,128]{1,0:T(8,128)}, f32[1920,128]{1,0:T(8,128)}, f32[1920,128]{1,0:T(8,128)}) fusion(f32[1920,128]{1,0:T(8,128)S(1)} %bitcast.11, f32[1920,128]{1,0:T(8,128)} %get-tuple-element.11, f32[1920,128]{1,0:T(8,128)S(1)} %bitcast.13, f32[1920,128]{1,0:T(8,128)} %bitcast.14), kind=kLoop, calls=%fused_computation.2 | loop fusion | flops 3686400 | bytes 6881280 | tf_op jit(solution)/shard_map/sub | solution.py:546
  138.7 0.0 copy-done.2
  138.7 0.6 copy.15
Async XLA Ops:
  0.6 134.5 %copy-start = (f32[48,1,5120]{2,1,0:T(1,128)S(1)}, f32[48,1,5120]{2,1,0:T(1,128)}, u32[]{:S(2)}) copy-start(f32[48,1,5120]{2,1,0:T(1,128)} %param.11) | copy-start | bytes 2949124
  0.6 134.5 %copy-start.1 = (f32[48,1,5120]{2,1,0:T(1,128)S(1)}, f32[48,1,5120]{2,1,0:T(1,128)}, u32[]{:S(2)}) copy-start(f32[48,1,5120]{2,1,0:T(1,128)} %param.12) | copy-start | bytes 2949124
  135.1 3.6 %copy-start.2 = (f32[16,128]{1,0:T(8,128)S(1)}, f32[16,128]{1,0:T(8,128)}, u32[]{:S(2)}) copy-start(f32[16,128]{1,0:T(8,128)} %get-tuple-element.13) | copy-start | bytes 24580

commit v6 on v5

--- a/solution.py
+++ b/solution.py
@@ -26,7 +26,7 @@
 FIRST = 9
 SINGLE = 2
 STRAIGHT = 2
-T_W, T_CODE, T_H1 = 1, 3, 7
+T_W, T_CODE, T_H1 = 1, 3, 6
 LAG_W = (1, 3)
 
 Z_OWN, XP_OWN, XM_OWN, SIB_OWN = 0, 1, 2, 3
@@ -39,8 +39,8 @@
 
 (R_A, R_Z, R_X, R_XF, R_SIB, R_WZ, R_WF, R_FZ, R_RZ, R_RY) = range(10)
 RECVS = 10
-(O_W, O_H, O_HF, O_C, O_G) = range(5)
-ONCE = 5
+(O_W, O_H, O_HS, O_HF, O_C, O_G) = range(6)
+ONCE = 6
 
 
 def kernel(
@@ -183,11 +183,14 @@
 
     def share_hidden():
         load_hidden.wait()
-        rc(ss.at[SH], os_.at[O_H], HB.at[y], HB.at[y], yp).start()
-        rc(ss.at[SH], os_.at[O_H], HB.at[y], HB.at[y], ym).start()
+        first, second = HB.at[y, 0 : rows // 2], HB.at[y, rows // 2 : rows]
+        rc(ss.at[SH], os_.at[O_H], first, first, yp).start()
+        rc(ss.at[SH], os_.at[O_H], second, second, ym).start()
+        rc(ss.at[SH], os_.at[O_HS], second, second, yp).start()
+        rc(ss.at[SH], os_.at[O_HS], first, first, ym).start()
 
     def hidden1():
-        arrive_once(O_H, HB.at[0:2])
+        arrive_once(O_H, HB.at[0])
         before, after = HB.at[down(y), 0 : rows // 2], HB.at[up(y), rows // 2 : rows]
         rc(ss.at[SHF], os_.at[O_HF], before, before, yp).start()
         rc(ss.at[SHF], os_.at[O_HF], after, after, ym).start()
@@ -223,6 +226,7 @@
         lax.fori_loop(0, NY, select, 0)
 
     def setup_hidden():
+        arrive_once(O_HS, HB.at[0])
         arrive_once(O_HF, HB.at[0])
         for yy in range(NY):
             HT[:, yy * rows : (yy + 1) * rows] = HB[yy].T

time: 139 us -> 140 us (level)
  no operation moved by 1% of the time
where the time goes in v6:
time: 140 us
  Pallas kernels  135 us (96%)
  other arithmetic  3.55 us (3%)
    pallas_call x1, Pallas kernels, exchange(): pl.pallas_call(kernel, out_shape=(jax.ShapeDtypeStruct(master.shape, F32)...  135 us
    sub x1, other arithmetic, shards(): master - learn_rate * (first_hat / (jnp.sqrt(second_hat) + epsilon) + dec...  3.55 us

profile of v6, /device:TPU:1, one launch (start us, length us, event | category | flops | bytes accessed | tf_op | source)
XLA Modules:
  0.0 140.2 jit_solution(6957013054059656952)
XLA Ops:
  0.6 0.0 copy-start
  0.6 0.0 copy-start.1
  0.7 135.4 %shard_map.102 = (f32[1920,128]{1,0:T(8,128)}, f32[16,128]{1,0:T(8,128)}) custom-call(bf16[128,5120]{1,0:T(8,128)(2,1)} %og_in.1, s32[6,128]{1,0:T(8,128)} %bitcast.20, f32[16,128]{1,0:T(8,128)} %bitcast.18, bf16[896,768]{1,0:T(8,128)(2,1)} %bitcast.12, f32[1920,128]{1,0:T(8,128)} %bitcast.10), custom_call_target="tpu_custom_call" | custom-call | tf_op jit(solution)/shard_map/pallas_call | solution.py:492
  136.1 0.0 copy-done
  136.1 0.0 copy-done.1
  136.1 0.0 copy-start.2
  136.1 3.5 %multiply_subtract_fusion = (f32[1920,128]{1,0:T(8,128)}, f32[1920,128]{1,0:T(8,128)}, f32[1920,128]{1,0:T(8,128)}) fusion(f32[1920,128]{1,0:T(8,128)S(1)} %bitcast.11, f32[1920,128]{1,0:T(8,128)} %get-tuple-element.11, f32[1920,128]{1,0:T(8,128)S(1)} %bitcast.13, f32[1920,128]{1,0:T(8,128)} %bitcast.14), kind=kLoop, calls=%fused_computation.2 | loop fusion | flops 3686400 | bytes 6881280 | tf_op jit(solution)/shard_map/sub | solution.py:550
  139.6 0.0 copy-done.2
  139.6 0.6 copy.15
Async XLA Ops:
  0.6 135.4 %copy-start = (f32[48,1,5120]{2,1,0:T(1,128)S(1)}, f32[48,1,5120]{2,1,0:T(1,128)}, u32[]{:S(2)}) copy-start(f32[48,1,5120]{2,1,0:T(1,128)} %param.11) | copy-start | bytes 2949124
  0.6 135.4 %copy-start.1 = (f32[48,1,5120]{2,1,0:T(1,128)S(1)}, f32[48,1,5120]{2,1,0:T(1,128)}, u32[]{:S(2)}) copy-start(f32[48,1,5120]{2,1,0:T(1,128)} %param.12) | copy-start | bytes 2949124
  136.1 3.6 %copy-start.2 = (f32[16,128]{1,0:T(8,128)S(1)}, f32[16,128]{1,0:T(8,128)}, u32[]{:S(2)}) copy-start(f32[16,128]{1,0:T(8,128)} %get-tuple-element.13) | copy-start | bytes 24580
